TPU v7x, 32 devices: a whole 2x2x4 slice. The times are simulated.
32 devices in a mesh: gx: 4 (over y, x), gy: 8 (over z, core).
Axes of the slice: x: 2, y: 2, z: 4, core: 2. Of those that a mesh axis runs over, the one named last changes fastest.
Arguments:
- populations: float32 [19, 64, 256, 256], P(None, 'gx', 'gy'), may hold values from 0.02 to 0.08
- ions: float32 [2, 64, 256, 256], P(None, 'gx', 'gy'), may hold values from 0.4 to 1.62, as said below
- mask: int32 [64, 256, 256], P('gx', 'gy'), may hold values from 0 to 1, as said below
Outputs:
- populations_out: float32 [19, 64, 256, 256], P(None, 'gx', 'gy')
- ions_out: float32 [2, 64, 256, 256], P(None, 'gx', 'gy')
- potential: float32 [64, 256, 256], P('gx', 'gy')
Inputs may be any that keep to these rules, and one draw needn't show every extreme that they name: `mask`: 1 marks a solid cell: every cell with second index 0 or 255 or third index 0 or 255, and scattered cells elsewhere; 0 marks fluid. `ions`: positive concentrations.
All inputs are finite; a program needn't handle non-finite values.
Results may differ from a plain program's by a relative error of at most 0.0004.
Values sent between devices are 32-bit elements; how exact they have to be, the bound alone decides.
A program may use at most 128 MiB of HBM per device.

v0:
```python
import math

import jax
import jax.numpy as jnp
import numpy as np
from jax import lax
from jax.experimental import pallas as pl
from jax.experimental.pallas import tpu as pltpu
from jax.sharding import PartitionSpec as P

PRECISE = lax.Precision.HIGH
C = [
    (0, 0, 0), (1, 0, 0), (-1, 0, 0), (0, 1, 0), (0, -1, 0), (0, 0, 1), (0, 0, -1),
    (1, 1, 0), (-1, -1, 0), (1, -1, 0), (-1, 1, 0), (1, 0, 1), (-1, 0, -1),
    (1, 0, -1), (-1, 0, 1), (0, 1, 1), (0, -1, -1), (0, 1, -1), (0, -1, 1),
]
WEIGHTS = [1.0 / 3.0] + [1.0 / 18.0] * 6 + [1.0 / 36.0] * 12
RELAXATION = 0.8
SCREENING = 0.001
WALL_CHARGE = -0.1
FIELD_EXT = 0.3
DIFFUSIVITY = 0.1
XP = [i for i in range(19) if C[i][0] == 1]
XM = [i for i in range(19) if C[i][0] == -1]
X0 = [i for i in range(19) if C[i][0] == 0]
YP = [i for i in range(19) if C[i][1] == 1]
YM = [i for i in range(19) if C[i][1] == -1]


def sine_table(n):
    s = np.arange(1, n + 1, dtype=np.int64)
    return np.sin((s[:, None] * s[None, :] % (2 * (n + 1))) * (math.pi / (n + 1))).astype(np.float32)


def hartley_table(n):
    s = np.arange(n, dtype=np.int64)
    a = (s[:, None] * s[None, :] % n) * (2.0 * math.pi / n)
    return ((np.cos(a) + np.sin(a)) / math.sqrt(n)).astype(np.float32)


def up(x, axis):
    n = lax.axis_size(axis)
    return lax.ppermute(x, axis, [(i, (i + 1) % n) for i in range(n)])


def down(x, axis):
    n = lax.axis_size(axis)
    return lax.ppermute(x, axis, [((i + 1) % n, i) for i in range(n)])


def shifted(x, step, axis):
    return pltpu.roll(x, step % x.shape[axis], axis)


def collide_kernel(pop, ion, fluid, pot, p0, pp, pm, ions_out):
    x = pl.program_id(0)
    rows, depth = 8, pop.shape[3]
    lane = lax.broadcasted_iota(jnp.int32, (rows, depth), 1)
    for j in range(pop.shape[2] // rows):
        lo = j * rows
        mid = pl.ds(lo + 1, rows)
        here = pl.ds(lo, rows)
        isf = fluid[x + 1, mid, :] > 0.0
        con = [ion[s, x + 1, mid, :] for s in range(2)]
        charge = jnp.where(isf, con[0] - con[1], WALL_CHARGE)
        phi = pot[x + 1, mid, :]
        after = jnp.where(lane == depth - 1, 0.0, shifted(phi, -1, 1))
        before = jnp.where(lane == 0, 0.0, shifted(phi, 1, 1))
        field = [
            FIELD_EXT - 0.5 * (pot[x + 2, mid, :] - pot[x, mid, :]),
            -0.5 * (pot[x + 1, pl.ds(lo + 2, rows), :] - pot[x + 1, pl.ds(lo, rows), :]),
            -0.5 * (after - before),
        ]
        load = jnp.where(isf, charge, 0.0)
        force = [load * f for f in field]
        f = [pop[i, 0, here, :] for i in range(19)]
        rho = f[0]
        for i in range(1, 19):
            rho = rho + f[i]
        inv = 1.0 / rho
        vel = []
        for a in range(3):
            m = 0.5 * force[a]
            for i in range(1, 19, 2):
                if C[i][a] == 1:
                    m = m + (f[i] - f[i + 1])
                elif C[i][a] == -1:
                    m = m - (f[i] - f[i + 1])
            vel.append(m * inv)
        r = rho * (1.0 / RELAXATION)
        half = 1.0 - 0.5 / RELAXATION
        speed = vel[0] * vel[0] + vel[1] * vel[1] + vel[2] * vel[2]
        power = vel[0] * force[0] + vel[1] * force[1] + vel[2] * force[2]
        base = r * (1.0 - 1.5 * speed) - (3.0 * half) * power
        keep = 1.0 - 1.0 / RELAXATION
        odd = [3.0 * r * vel[a] + (3.0 * half) * force[a] for a in range(3)]
        even = [4.5 * r * vel[a] + (9.0 * half) * force[a] for a in range(3)]

        def put(i, value):
            if i in XP:
                pp[XP.index(i), 0, here, :] = value
            elif i in XM:
                pm[XM.index(i), 0, here, :] = value
            else:
                p0[X0.index(i), 0, here, :] = value

        def along(c, v):
            total = None
            for a in range(3):
                if c[a] == 1:
                    total = v[a] if total is None else total + v[a]
                elif c[a] == -1:
                    total = -v[a] if total is None else total - v[a]
            return total

        put(0, jnp.where(isf, keep * f[0] + WEIGHTS[0] * base, f[0]))
        for i in range(1, 19, 2):
            e = WEIGHTS[i] * (base + along(C[i], vel) * along(C[i], even))
            o = WEIGHTS[i] * along(C[i], odd)
            put(i, jnp.where(isf, keep * f[i] + (e + o), f[i + 1]))
            put(i + 1, jnp.where(isf, keep * f[i + 1] + (e - o), f[i]))

        fl = fluid[x + 1, mid, :]
        near = [
            ((x + 2, mid), (x, mid)),
            ((x + 1, pl.ds(lo + 2, rows)), (x + 1, pl.ds(lo, rows))),
        ]
        flags = [[fluid[p, q, :] > 0.0 for p, q in pair] for pair in near]
        flags.append([shifted(fl, -1, 1) > 0.0, shifted(fl, 1, 1) > 0.0])
        for s in range(2):
            sign = 1.0 - 2.0 * s
            c = con[s]
            lap = -6.0 * c
            drift = c * (SCREENING * phi - charge)
            adv = 0.0
            for a in range(3):
                if a < 2:
                    q = [ion[s, pa, pb, :] for pa, pb in near[a]]
                else:
                    q = [shifted(c, -1, 1), shifted(c, 1, 1)]
                u = jnp.where(flags[a][0], q[0], c)
                d = jnp.where(flags[a][1], q[1], c)
                lap = lap + u + d
                slope = 0.5 * (u - d)
                drift = drift - slope * field[a]
                adv = adv + slope * vel[a]
            change = DIFFUSIVITY * (lap + sign * drift) - adv
            ions_out[s, 0, here, :] = jnp.where(isf, c + change, c)


def stream_kernel(p0, pp, pm, hl, hr, hb, ht, out):
    x = pl.program_id(0)
    last = pl.num_programs(0) - 1
    wid, depth = out.shape[2], out.shape[3]
    row = lax.broadcasted_iota(jnp.int32, (wid, depth), 0)
    for i in range(19):
        if i in XP:
            k = XP.index(i)
            plane = jnp.where(x == 0, hl[k], pp[k, 0])
        elif i in XM:
            k = XM.index(i)
            plane = jnp.where(x == last, hr[k], pm[k, 0])
        else:
            plane = p0[X0.index(i), 0]
        if C[i][1] == 1:
            halo = hb[YP.index(i), pl.ds(x, 1), :]
            plane = jnp.where(row == 0, halo, shifted(plane, 1, 0))
        elif C[i][1] == -1:
            halo = ht[YM.index(i), pl.ds(x, 1), :]
            plane = jnp.where(row == wid - 1, halo, shifted(plane, -1, 0))
        if C[i][2] != 0:
            plane = shifted(plane, C[i][2], 1)
        out[i, 0] = plane


def solve(charge):
    length, wid, depth = charge.shape
    gx, gy = lax.axis_size("gx"), lax.axis_size("gy")
    parts = gx * gy
    modes = depth // parts
    sz, sy, hx = sine_table(depth), sine_table(wid * gy), hartley_table(length * gx)
    full_len, full_wid = length * gx, wid * gy
    t = jnp.einsum("nz,pz->np", sz, charge.reshape(length * wid, depth), precision=PRECISE)
    t = t.reshape(parts, modes, length * wid)
    t = lax.all_to_all(t, ("gx", "gy"), split_axis=0, concat_axis=0, tiled=True)
    t = t.reshape(gx, gy, modes, length, wid).transpose(2, 0, 3, 1, 4)
    t = t.reshape(modes, full_len, full_wid)
    t = jnp.einsum("nxy,my->nxm", t, sy, precision=PRECISE)
    t = jnp.einsum("kx,nxm->nkm", hx, t, precision=PRECISE)
    me = lax.axis_index("gx") * gy + lax.axis_index("gy")

    def wall(first, number, total):
        m = (jnp.arange(number, dtype=jnp.int32) + first + 1).astype(jnp.float32)
        return 2.0 - 2.0 * jnp.cos(m * (math.pi / (total + 1)))

    ex = (2.0 - 2.0 * np.cos(np.arange(full_len) * (2.0 * math.pi / full_len))).astype(np.float32)
    denom = (
        SCREENING
        + ex[None, :, None]
        + wall(0, full_wid, full_wid)[None, None, :]
        + wall(me * modes, modes, depth)[:, None, None]
    )
    t = t * ((4.0 / ((full_wid + 1) * (depth + 1))) / denom)
    t = jnp.einsum("kx,nkm->nxm", hx, t, precision=PRECISE)
    t = jnp.einsum("nxm,my->nxy", t, sy, precision=PRECISE)
    t = t.reshape(modes, gx, length, gy, wid).transpose(1, 3, 0, 2, 4)
    t = t.reshape(parts, modes, length * wid)
    t = lax.all_to_all(t, ("gx", "gy"), split_axis=0, concat_axis=0, tiled=True)
    t = t.reshape(depth, length * wid)
    return jnp.einsum("np,nz->pz", t, sz, precision=PRECISE).reshape(length, wid, depth)


def beside(block, keep_low, keep_high):
    d = block.ndim
    cut = lambda v, lo, hi, axis: lax.slice_in_dim(v, lo, hi, axis=axis)
    lx, ly = block.shape[d - 3], block.shape[d - 2]
    left = up(cut(block, lx - 1, lx, d - 3), "gx")
    right = down(cut(block, 0, 1, d - 3), "gx")
    low = up(cut(block, ly - 1, ly, d - 2), "gy") * keep_low
    high = down(cut(block, 0, 1, d - 2), "gy") * keep_high
    mid = jnp.concatenate([low, block, high], axis=d - 2)
    pad = [(0, 0)] * (d - 3) + [(0, 0), (1, 1), (0, 0)]
    return jnp.concatenate([jnp.pad(left, pad), mid, jnp.pad(right, pad)], axis=d - 3)


def body(populations, ions, mask):
    length, wid, depth = mask.shape
    ygo = lax.axis_index("gy")
    fluid = (mask == 0).astype(jnp.float32)
    charge = fluid * (ions[0] - ions[1]) + (1.0 - fluid) * WALL_CHARGE
    ionic = beside(jnp.concatenate([ions, fluid[None]], axis=0), 1.0, 1.0)
    potential = solve(charge)
    pot = beside(
        potential,
        (ygo != 0).astype(jnp.float32),
        (ygo != lax.axis_size("gy") - 1).astype(jnp.float32),
    )
    block = lambda n, f: pl.BlockSpec((n, 1, wid, depth), lambda x: (0, f(x), 0, 0))
    same = lambda x: x
    whole = pl.BlockSpec(memory_space=pltpu.VMEM)
    shape = lambda n: jax.ShapeDtypeStruct((n, length, wid, depth), jnp.float32)
    cells = length * wid * depth
    p0, pp, pm, ions_out = pl.pallas_call(
        collide_kernel,
        grid=(length,),
        in_specs=[block(19, same), whole, whole, whole],
        out_specs=[block(9, same), block(5, same), block(5, same), block(2, same)],
        out_shape=[shape(9), shape(5), shape(5), shape(2)],
        compiler_params=pltpu.CompilerParams(vmem_limit_bytes=32 << 20),
        cost_estimate=pl.CostEstimate(
            flops=500 * cells, bytes_accessed=4 * 44 * cells, transcendentals=0
        ),
    )(populations, ionic[:2], ionic[2], pot)

    hl = up(pp[:, length - 1], "gx")
    hr = down(pm[:, 0], "gx")

    def row(i, y):
        if i in XP:
            return pp[XP.index(i), :, y]
        if i in XM:
            return pm[XM.index(i), :, y]
        return p0[X0.index(i), :, y]

    def moved(i, rows, beside_left, beside_right):
        if i in XP:
            return jnp.concatenate([beside_left, rows[:-1]], axis=0)
        if i in XM:
            return jnp.concatenate([rows[1:], beside_right], axis=0)
        return rows

    def rows_of(group, y):
        out = []
        for i in group:
            a = hl[XP.index(i), y][None] if i in XP else None
            b = hr[XM.index(i), y][None] if i in XM else None
            out.append(moved(i, row(i, y), a, b))
        return jnp.stack(out)

    hb = up(rows_of(YP, wid - 1), "gy")
    ht = down(rows_of(YM, 0), "gy")
    populations_out = pl.pallas_call(
        stream_kernel,
        grid=(length,),
        in_specs=[
            block(9, same),
            block(5, lambda x: jnp.maximum(x - 1, 0)),
            block(5, lambda x: jnp.minimum(x + 1, length - 1)),
            whole,
            whole,
            whole,
            whole,
        ],
        out_specs=block(19, same),
        out_shape=shape(19),
        compiler_params=pltpu.CompilerParams(vmem_limit_bytes=32 << 20),
        cost_estimate=pl.CostEstimate(
            flops=20 * cells, bytes_accessed=4 * 38 * cells, transcendentals=0
        ),
    )(p0, pp, pm, hl, hr, hb, ht)
    return populations_out, ions_out, potential


def solution(mesh):
    placed = (P(None, "gx", "gy", None), P(None, "gx", "gy", None), P("gx", "gy", None))
    return jax.shard_map(body, mesh=mesh, in_specs=placed, out_specs=placed, check_vma=False)
```

profile of v0, /device:TPU:0, one launch (start us, length us, event | category | flops | bytes accessed | tf_op | source)
XLA Modules:
  0.0 114.1 jit_solution(15823751395252786021)
XLA Ops:
  0.7 1.6 %fusion.2 = (f32[16,32,256]{2,1,0:T(8,128)S(1)}, pred[16,32,256]{2,1,0:T(8,128)(4,1)S(1)}) fusion(f32[2,16,32,256]{3,2,1,0:T(8,128)} %param.11, s32[16,32,256]{2,1,0:T(8,128)} %param.12), kind=kLoop, calls=%fused_computation.17 | loop fusion | flops 917504 | bytes 2228224 | tf_op jit(solution)/shard_map/add | solution.py:230
  3.5 7.3 %all-to-all-start = ((f32[32,8,512]{2,1,0:T(8,128)}), f32[32,8,512]{2,1,0:T(8,128)S(1)}, u32[]{:S(2)}, u32[]{:S(2)}) async-start(f32[32,8,512]{2,1,0:T(8,128)} %convolution_bitcast_fusion.2), calls=%async_computation | async-start | bytes 1048576 | tf_op jit(solution)/shard_map/all_to_all | solution.py:185
  11.0 16.2 %all-to-all-done = f32[32,8,512]{2,1,0:T(8,128)S(1)} async-done(((f32[32,8,512]{2,1,0:T(8,128)}), f32[32,8,512]{2,1,0:T(8,128)S(1)}, u32[]{:S(2)}, u32[]{:S(2)}) %all-to-all-start) | async-done | bytes 524320 | tf_op jit(solution)/shard_map/all_to_all | solution.py:185
  27.7 2.5 %copy.38 = f32[8,4,16,8,32]{4,3,2,1,0:T(8,128)} copy(f32[8,4,16,8,32]{4,2,0,3,1:T(8,128)S(1)} %bitcast.111) | data formatting | bytes 1048576 | tf_op jit(solution)/shard_map/transpose | solution.py:186
  30.2 2.2 %reshape.92 = f32[8,64,256]{2,1,0:T(8,128)S(1)} reshape(f32[8,4,16,8,32]{4,3,2,1,0:T(8,128)} %copy.38) | data formatting | bytes 1048576 | tf_op jit(solution)/shard_map/reshape | solution.py:187
  34.5 1.7 %copy.60 = f32[8,4,16,8,32]{4,2,0,3,1:T(8,128)} copy(f32[8,4,16,8,32]{4,3,2,1,0:T(8,128)S(1)} %reshape.93) | data formatting | bytes 1048576 | tf_op jit(solution)/shard_map/reshape | solution.py:206
  36.2 3.0 %reshape.94 = f32[32,8,512]{2,1,0:T(8,128)} reshape(f32[4,8,8,16,32]{4,3,2,1,0:T(8,128)} %bitcast.112) | data formatting | bytes 1048576 | tf_op jit(solution)/shard_map/reshape | solution.py:207
  39.3 2.6 %all-to-all-start.1 = ((f32[32,8,512]{2,1,0:T(8,128)}), f32[32,8,512]{2,1,0:T(8,128)S(1)}, u32[]{:S(2)}, u32[]{:S(2)}) async-start(f32[32,8,512]{2,1,0:T(8,128)} %reshape.94), calls=%async_computation.1 | async-start | bytes 1048576 | tf_op jit(solution)/shard_map/all_to_all | solution.py:208
  42.0 1.7 %collective-permute-start = (f32[3,1,32,256]{3,2,1,0:T(8,128)S(1)}, f32[3,1,32,256]{3,2,1,0:T(8,128)S(1)}, u32[]{:S(2)}, u32[]{:S(2)}) collective-permute-start(f32[3,1,32,256]{3,2,1,0:T(8,128)S(1)} %get-tuple-element.25), channel_id=1, source_target_pairs={{0,8},{8,16},{16,24},{24,0},{1,9},{9,17},{17,25},{25,1},{2,10},{10... | collective-permute-start | bytes 294920 | tf_op jit(solution)/shard_map/ppermute | solution.py:43
  45.1 3.5 %collective-permute-start.2 = (f32[3,16,1,256]{3,2,1,0:T(1,128)S(1)}, f32[3,16,1,256]{3,2,1,0:T(1,128)S(1)}, u32[]{:S(2)}, u32[]{:S(2)}) collective-permute-start(f32[3,16,1,256]{3,2,1,0:T(1,128)S(1)} %get-tuple-element.24), channel_id=1, source_target_pairs={{1,0},{2,1},{3,2},{4,3},{5,4},{6,5},{7,6},{0,7},{9,8},{10,9},{11,1... | collective-permute-start | bytes 147464 | tf_op jit(solution)/shard_map/ppermute | solution.py:48
  48.6 7.0 %collective-permute-done.1 = f32[3,16,1,256]{3,2,1,0:T(1,128)S(1)} collective-permute-done((f32[3,16,1,256]{3,2,1,0:T(1,128)S(1)}, f32[3,16,1,256]{3,2,1,0:T(1,128)S(1)}, u32[]{:S(2)}, u32[]{:S(2)}) %collective-permute-start.1) | collective-permute-done | bytes 49184 | tf_op jit(solution)/shard_map/ppermute | solution.py:43
  56.1 2.7 %all-to-all-done.1 = f32[32,8,512]{2,1,0:T(8,128)S(1)} async-done(((f32[32,8,512]{2,1,0:T(8,128)}), f32[32,8,512]{2,1,0:T(8,128)S(1)}, u32[]{:S(2)}, u32[]{:S(2)}) %all-to-all-start.1) | async-done | bytes 524320 | tf_op jit(solution)/shard_map/all_to_all | solution.py:208
  59.5 3.5 %collective-permute-start.6 = (f32[16,1,256]{2,1,0:T(1,128)S(1)}, f32[16,1,256]{2,1,0:T(1,128)S(1)}, u32[]{:S(2)}, u32[]{:S(2)}) collective-permute-start(f32[16,1,256]{2,1,0:T(1,128)S(1)} %get-tuple-element.28), channel_id=1, source_target_pairs={{1,0},{2,1},{3,2},{4,3},{5,4},{6,5},{7,6},{0,7},{9,8},{10,9},{11,1... | collective-permute-start | bytes 49160 | tf_op jit(solution)/shard_map/ppermute | solution.py:48
  63.0 2.9 %collective-permute-start.7 = (f32[1,32,256]{2,1,0:T(8,128)S(1)}, f32[1,32,256]{2,1,0:T(8,128)S(1)}, u32[]{:S(2)}, u32[]{:S(2)}) collective-permute-start(f32[1,32,256]{2,1,0:T(8,128)S(1)} %get-tuple-element.30), channel_id=1, source_target_pairs={{8,0},{16,8},{24,16},{0,24},{9,1},{17,9},{25,17},{1,25},{10,2},{18... | collective-permute-start | bytes 98312 | tf_op jit(solution)/shard_map/ppermute | solution.py:48
  66.0 1.9 %collective-permute-done.4 = f32[1,32,256]{2,1,0:T(8,128)S(1)} collective-permute-done((f32[1,32,256]{2,1,0:T(8,128)S(1)}, f32[1,32,256]{2,1,0:T(8,128)S(1)}, u32[]{:S(2)}, u32[]{:S(2)}) %collective-permute-start.4) | collective-permute-done | bytes 32800 | tf_op jit(solution)/shard_map/ppermute | solution.py:43
  68.0 3.8 %copy-done = f32[19,16,32,256]{3,2,1,0:T(8,128)S(1)} copy-done((f32[19,16,32,256]{3,2,1,0:T(8,128)S(1)}, f32[19,16,32,256]{3,2,1,0:T(8,128)}, u32[]{:S(2)}) %copy-start) | copy-done | bytes 9961496
  71.8 15.5 %shard_map.121 = (f32[9,16,32,256]{3,2,1,0:T(8,128)S(1)}, f32[5,16,32,256]{3,2,1,0:T(8,128)S(1)}, f32[5,16,32,256]{3,2,1,0:T(8,128)S(1)}, f32[2,16,32,256]{3,2,1,0:T(8,128)}) custom-call(f32[19,16,32,256]{3,2,1,0:T(8,128)S(1)} %copy-done, f32[2,18,34,256]{3,2,1,0:T(8,128)S(1)} %slice.144.ion, f32[18,34,256]{2,1,0:T(8,128)S(1)} %slice_bitcast_fusion.fluid, ...), custom_call_target="tpu_custom_call" | custom-call | flops 65536000 | bytes 23068672 | tf_op jit(solution)/shard_map/pallas_call | solution.py:243
  87.3 1.5 %copy.44 = f32[5,16,32,256]{3,1,2,0:T(8,128)S(1)} copy(f32[5,16,32,256]{3,2,1,0:T(8,128)S(1)} %get-tuple-element.8.pp) | data formatting | bytes 5242880 | tf_op jit(solution)/shard_map/pallas_call | solution.py:243
  90.3 3.0 %collective-permute-start.9 = (f32[5,32,256]{2,1,0:T(8,128)S(1)}, f32[5,32,256]{2,1,0:T(8,128)S(1)}, u32[]{:S(2)}, u32[]{:S(2)}) collective-permute-start(f32[5,32,256]{2,1,0:T(8,128)S(1)} %slice_bitcast_fusion.1), channel_id=1, source_target_pairs={{8,0},{16,8},{24,16},{0,24},{9,1},{17,9},{25,17},{1,25},{10,2},{18... | collective-permute-start | bytes 491528 | tf_op jit(solution)/shard_map/ppermute | solution.py:48
  93.3 2.8 %copy.43 = f32[9,16,32,256]{3,1,2,0:T(8,128)S(1)} copy(f32[9,16,32,256]{3,2,1,0:T(8,128)S(1)} %get-tuple-element.7.p0) | data formatting | bytes 9437184 | tf_op jit(solution)/shard_map/pallas_call | solution.py:243
  96.1 3.3 %collective-permute-done.8.hl = f32[5,32,256]{2,1,0:T(8,128)S(1)} collective-permute-done((f32[5,32,256]{2,1,0:T(8,128)S(1)}, f32[5,32,256]{2,1,0:T(8,128)S(1)}, u32[]{:S(2)}, u32[]{:S(2)}) %collective-permute-start.8) | collective-permute-done | bytes 163872 | tf_op jit(solution)/shard_map/ppermute | solution.py:43
  100.1 2.1 %collective-permute-done.11.ht = f32[5,16,256]{2,1,0:T(8,128)S(1)} collective-permute-done((f32[5,16,256]{2,1,0:T(8,128)S(1)}, f32[5,16,256]{2,1,0:T(8,128)S(1)}, u32[]{:S(2)}, u32[]{:S(2)}) %collective-permute-start.11) | collective-permute-done | bytes 81952 | tf_op jit(solution)/shard_map/ppermute | solution.py:48
  102.2 3.4 %collective-permute-done.10.hb = f32[5,16,256]{2,1,0:T(8,128)S(1)} collective-permute-done((f32[5,16,256]{2,1,0:T(8,128)S(1)}, f32[5,16,256]{2,1,0:T(8,128)S(1)}, u32[]{:S(2)}, u32[]{:S(2)}) %collective-permute-start.10) | collective-permute-done | bytes 81952 | tf_op jit(solution)/shard_map/ppermute | solution.py:43
  105.6 8.5 %shard_map.122 = f32[19,16,32,256]{3,2,1,0:T(8,128)} custom-call(f32[9,16,32,256]{3,2,1,0:T(8,128)S(1)} %get-tuple-element.7.p0, f32[5,16,32,256]{3,2,1,0:T(8,128)S(1)} %get-tuple-element.8.pp, f32[5,16,32,256]{3,2,1,0:T(8,128)S(1)} %get-tuple-element.9.pm, f32[5,32,256]{2,1,0:T(8,128)S(1)} %collective-permute-done.8.hl, ...), custom_call_target="tpu_custom_call" | custom-call | flops 2621440 | bytes 19922944 | tf_op jit(solution)/shard_map/pallas_call | solution.py:282
  (62 shorter events, 8.9 us)
Async XLA Ops:
  0.6 1.6 %copy-start.3 = (f32[256,256]{1,0:T(8,128)S(1)}, f32[256,256]{1,0:T(8,128)}, u32[]{:S(2)}) copy-start(f32[256,256]{1,0:T(8,128)} %constant.39.clone) | copy-start | bytes 786436
  0.6 10.3 %copy-start.6 = (f32[64]{0:T(128)S(1)}, f32[64]{0:T(128)}, u32[]{:S(2)}) copy-start(f32[64]{0:T(128)} %constant.50) | copy-start | bytes 772
  3.5 23.7 %all-to-all-start = ((f32[32,8,512]{2,1,0:T(8,128)}), f32[32,8,512]{2,1,0:T(8,128)S(1)}, u32[]{:S(2)}, u32[]{:S(2)}) async-start(f32[32,8,512]{2,1,0:T(8,128)} %convolution_bitcast_fusion.2), calls=%async_computation | async-start | bytes 1048576 | tf_op jit(solution)/shard_map/all_to_all | solution.py:185
  30.2 2.2 %copy-start.4 = (f32[256,256,1]{1,0,2:T(8,128)S(1)}, f32[256,256,1]{1,0,2:T(8,128)}, u32[]{:S(2)}) copy-start(f32[256,256,1]{1,0,2:T(8,128)} %constant.51) | copy-start | bytes 786436
  30.2 2.6 %copy-start.5 = (f32[64,64,1]{1,0,2:T(8,128)S(1)}, f32[64,64,1]{1,0,2:T(8,128)}, u32[]{:S(2)}) copy-start(f32[64,64,1]{1,0,2:T(8,128)} %constant.52) | copy-start | bytes 49156
  36.2 5.7 %copy-start.1 = (f32[2,16,32,256]{3,2,1,0:T(8,128)S(1)}, f32[2,16,32,256]{3,2,1,0:T(8,128)}, u32[]{:S(2)}) copy-start(f32[2,16,32,256]{3,2,1,0:T(8,128)} %param.11) | copy-start | bytes 3145732
  39.3 19.5 %all-to-all-start.1 = ((f32[32,8,512]{2,1,0:T(8,128)}), f32[32,8,512]{2,1,0:T(8,128)S(1)}, u32[]{:S(2)}, u32[]{:S(2)}) async-start(f32[32,8,512]{2,1,0:T(8,128)} %reshape.94), calls=%async_computation.1 | async-start | bytes 1048576 | tf_op jit(solution)/shard_map/all_to_all | solution.py:208
  42.0 13.6 %collective-permute-start = (f32[3,1,32,256]{3,2,1,0:T(8,128)S(1)}, f32[3,1,32,256]{3,2,1,0:T(8,128)S(1)}, u32[]{:S(2)}, u32[]{:S(2)}) collective-permute-start(f32[3,1,32,256]{3,2,1,0:T(8,128)S(1)} %get-tuple-element.25), channel_id=1, source_target_pairs={{0,8},{8,16},{16,24},{24,0},{1,9},{9,17},{17,25},{25,1},{2,10},{10... | collective-permute-start | bytes 294920 | tf_op jit(solution)/shard_map/ppermute | solution.py:43
  43.7 12.0 %collective-permute-start.3 = (f32[3,1,32,256]{3,2,1,0:T(8,128)S(1)}, f32[3,1,32,256]{3,2,1,0:T(8,128)S(1)}, u32[]{:S(2)}, u32[]{:S(2)}) collective-permute-start(f32[3,1,32,256]{3,2,1,0:T(8,128)S(1)} %get-tuple-element.26), channel_id=1, source_target_pairs={{8,0},{16,8},{24,16},{0,24},{9,1},{17,9},{25,17},{1,25},{10,2},{18... | collective-permute-start | bytes 294920 | tf_op jit(solution)/shard_map/ppermute | solution.py:48
  45.0 10.6 %collective-permute-start.1 = (f32[3,16,1,256]{3,2,1,0:T(1,128)S(1)}, f32[3,16,1,256]{3,2,1,0:T(1,128)S(1)}, u32[]{:S(2)}, u32[]{:S(2)}) collective-permute-start(f32[3,16,1,256]{3,2,1,0:T(1,128)S(1)} %get-tuple-element.23), channel_id=1, source_target_pairs={{0,1},{1,2},{2,3},{3,4},{4,5},{5,6},{6,7},{7,0},{8,9},{9,10},{10,1... | collective-permute-start | bytes 147464 | tf_op jit(solution)/shard_map/ppermute | solution.py:43
  45.1 10.5 %collective-permute-start.2 = (f32[3,16,1,256]{3,2,1,0:T(1,128)S(1)}, f32[3,16,1,256]{3,2,1,0:T(1,128)S(1)}, u32[]{:S(2)}, u32[]{:S(2)}) collective-permute-start(f32[3,16,1,256]{3,2,1,0:T(1,128)S(1)} %get-tuple-element.24), channel_id=1, source_target_pairs={{1,0},{2,1},{3,2},{4,3},{5,4},{6,5},{7,6},{0,7},{9,8},{10,9},{11,1... | collective-permute-start | bytes 147464 | tf_op jit(solution)/shard_map/ppermute | solution.py:48
  59.4 27.9 %copy-start.2 = (f32[512,256]{1,0:T(8,128)}, f32[512,256]{1,0:T(8,128)S(1)}, u32[]{:S(2)}) copy-start(f32[512,256]{1,0:T(8,128)S(1)} %fusion.3) | copy-start | bytes 1572868
  59.4 6.5 %collective-permute-start.5 = (f32[16,1,256]{2,1,0:T(1,128)S(1)}, f32[16,1,256]{2,1,0:T(1,128)S(1)}, u32[]{:S(2)}, u32[]{:S(2)}) collective-permute-start(f32[16,1,256]{2,1,0:T(1,128)S(1)} %get-tuple-element.27), channel_id=1, source_target_pairs={{0,1},{1,2},{2,3},{3,4},{4,5},{5,6},{6,7},{7,0},{8,9},{9,10},{10,1... | collective-permute-start | bytes 49160 | tf_op jit(solution)/shard_map/ppermute | solution.py:43
  59.5 6.5 %collective-permute-start.6 = (f32[16,1,256]{2,1,0:T(1,128)S(1)}, f32[16,1,256]{2,1,0:T(1,128)S(1)}, u32[]{:S(2)}, u32[]{:S(2)}) collective-permute-start(f32[16,1,256]{2,1,0:T(1,128)S(1)} %get-tuple-element.28), channel_id=1, source_target_pairs={{1,0},{2,1},{3,2},{4,3},{5,4},{6,5},{7,6},{0,7},{9,8},{10,9},{11,1... | collective-permute-start | bytes 49160 | tf_op jit(solution)/shard_map/ppermute | solution.py:48
  63.0 4.8 %collective-permute-start.4 = (f32[1,32,256]{2,1,0:T(8,128)S(1)}, f32[1,32,256]{2,1,0:T(8,128)S(1)}, u32[]{:S(2)}, u32[]{:S(2)}) collective-permute-start(f32[1,32,256]{2,1,0:T(8,128)S(1)} %get-tuple-element.29), channel_id=1, source_target_pairs={{0,8},{8,16},{16,24},{24,0},{1,9},{9,17},{17,25},{25,1},{2,10},{10... | collective-permute-start | bytes 98312 | tf_op jit(solution)/shard_map/ppermute | solution.py:43
  63.0 4.8 %collective-permute-start.7 = (f32[1,32,256]{2,1,0:T(8,128)S(1)}, f32[1,32,256]{2,1,0:T(8,128)S(1)}, u32[]{:S(2)}, u32[]{:S(2)}) collective-permute-start(f32[1,32,256]{2,1,0:T(8,128)S(1)} %get-tuple-element.30), channel_id=1, source_target_pairs={{8,0},{16,8},{24,16},{0,24},{9,1},{17,9},{25,17},{1,25},{10,2},{18... | collective-permute-start | bytes 98312 | tf_op jit(solution)/shard_map/ppermute | solution.py:48
  68.0 3.8 %copy-start = (f32[19,16,32,256]{3,2,1,0:T(8,128)S(1)}, f32[19,16,32,256]{3,2,1,0:T(8,128)}, u32[]{:S(2)}) copy-start(f32[19,16,32,256]{3,2,1,0:T(8,128)} %pop.1) | copy-start | bytes 29884420
  90.3 5.8 %collective-permute-start.9 = (f32[5,32,256]{2,1,0:T(8,128)S(1)}, f32[5,32,256]{2,1,0:T(8,128)S(1)}, u32[]{:S(2)}, u32[]{:S(2)}) collective-permute-start(f32[5,32,256]{2,1,0:T(8,128)S(1)} %slice_bitcast_fusion.1), channel_id=1, source_target_pairs={{8,0},{16,8},{24,16},{0,24},{9,1},{17,9},{25,17},{1,25},{10,2},{18... | collective-permute-start | bytes 491528 | tf_op jit(solution)/shard_map/ppermute | solution.py:48
  93.3 6.2 %collective-permute-start.8 = (f32[5,32,256]{2,1,0:T(8,128)S(1)}, f32[5,32,256]{2,1,0:T(8,128)S(1)}, u32[]{:S(2)}, u32[]{:S(2)}) collective-permute-start(f32[5,32,256]{2,1,0:T(8,128)S(1)} %slice_bitcast_fusion.2), channel_id=1, source_target_pairs={{0,8},{8,16},{16,24},{24,0},{1,9},{9,17},{17,25},{25,1},{2,10},{10... | collective-permute-start | bytes 491528 | tf_op jit(solution)/shard_map/ppermute | solution.py:43
  99.5 2.7 %collective-permute-start.11 = (f32[5,16,256]{2,1,0:T(8,128)S(1)}, f32[5,16,256]{2,1,0:T(8,128)S(1)}, u32[]{:S(2)}, u32[]{:S(2)}) collective-permute-start(f32[5,16,256]{2,1,0:T(8,128)S(1)} %get-tuple-element.13), channel_id=1, source_target_pairs={{1,0},{2,1},{3,2},{4,3},{5,4},{6,5},{7,6},{0,7},{9,8},{10,9},{11,1... | collective-permute-start | bytes 245768 | tf_op jit(solution)/shard_map/ppermute | solution.py:48
  100.0 5.7 %collective-permute-start.10 = (f32[5,16,256]{2,1,0:T(8,128)S(1)}, f32[5,16,256]{2,1,0:T(8,128)S(1)}, u32[]{:S(2)}, u32[]{:S(2)}) collective-permute-start(f32[5,16,256]{2,1,0:T(8,128)S(1)} %get-tuple-element.14), channel_id=1, source_target_pairs={{0,1},{1,2},{2,3},{3,4},{4,5},{5,6},{6,7},{7,0},{8,9},{9,10},{10,1... | collective-permute-start | bytes 245768 | tf_op jit(solution)/shard_map/ppermute | solution.py:43
where the time goes:
time: 114 us
  waiting for transfers between devices  36.6 us (32%)
  starting transfers between devices  26.5 us (23%)
  Pallas kernels  24 us (21%)
  local copies, waits for them, and re-layouts  20.3 us (18%)
  matrix products  3.43 us (3%)
  other arithmetic  2.32 us (2%)
    all_to_all x2, waiting for transfers between devices, solve(): t = lax.all_to_all(t, ('gx', 'gy'), split_axis=0, concat_axis=0, tiled=True)  18.8 us
    ppermute x6, waiting for transfers between devices, up(): return lax.ppermute(x, axis, [(i, (i + 1) % n) for i in range(n)])  15.6 us
    pallas_call x1, Pallas kernels, body(): pl.pallas_call(collide_kernel, grid=(length,), in_specs=[block(19, same),...  15.5 us
    ppermute x6, starting transfers between devices, down(): return lax.ppermute(x, axis, [((i + 1) % n, i) for i in range(n)])  14.7 us
    all_to_all x2, starting transfers between devices, solve(): t = lax.all_to_all(t, ('gx', 'gy'), split_axis=0, concat_axis=0, tiled=True)  9.9 us
    pallas_call x1, Pallas kernels, body(): pl.pallas_call(stream_kernel, grid=(length,), in_specs=[block(9, same), b...  8.51 us
    pallas_call x3, local copies, waits for them, and re-layouts, body(): pl.pallas_call(collide_kernel, grid=(length,), in_specs=[block(19, same),...  5.78 us
    unnamed x16, local copies, waits for them, and re-layouts  3.87 us
  transfers between devices with their start and end apart: 14, of which 7 were waited for; matrix products, arithmetic and copies ran while one was open for 3% of the time, Pallas kernels for 0%

commit v1 on v0

--- a/solution.py
+++ b/solution.py
@@ -1,3 +1,4 @@
+import functools
 import math
 
 import jax
@@ -52,8 +53,21 @@
     return pltpu.roll(x, step % x.shape[axis], axis)
 
 
-def collide_kernel(pop, ion, fluid, pot, p0, pp, pm, ions_out):
-    x = pl.program_id(0)
+def collide_kernel(pop, ion, fluid, pot, p0, pp, pm, ions_out, top, bottom):
+    collide_plane(pl.program_id(0), pop, ion, fluid, pot, p0, pp, pm, ions_out, top, bottom)
+
+
+def faces_kernel(length, pop, ion, fluid, pot, face_p, face_m):
+    @pl.when(pl.program_id(0) == 0)
+    def _():
+        collide_plane(0, pop, ion, fluid, pot, None, None, face_m, None, None, None)
+
+    @pl.when(pl.program_id(0) == 1)
+    def _():
+        collide_plane(length - 1, pop, ion, fluid, pot, None, face_p, None, None, None, None)
+
+
+def collide_plane(x, pop, ion, fluid, pot, p0, pp, pm, ions_out, top, bottom):
     rows, depth = 8, pop.shape[3]
     lane = lax.broadcasted_iota(jnp.int32, (rows, depth), 1)
     for j in range(pop.shape[2] // rows):
@@ -97,12 +111,14 @@
         even = [4.5 * r * vel[a] + (9.0 * half) * force[a] for a in range(3)]
 
         def put(i, value):
-            if i in XP:
-                pp[XP.index(i), 0, here, :] = value
-            elif i in XM:
-                pm[XM.index(i), 0, here, :] = value
-            else:
-                p0[X0.index(i), 0, here, :] = value
+            ref, group = (pp, XP) if i in XP else (pm, XM) if i in XM else (p0, X0)
+            if ref is None:
+                return
+            ref[group.index(i), 0, here, :] = value
+            if top is not None and i in YP and lo + rows == pop.shape[2]:
+                top[YP.index(i), pl.ds(x, 1), :] = value[rows - 1 : rows]
+            if bottom is not None and i in YM and lo == 0:
+                bottom[YM.index(i), pl.ds(x, 1), :] = value[0:1]
 
         def along(c, v):
             total = None
@@ -120,6 +136,8 @@
             put(i, jnp.where(isf, keep * f[i] + (e + o), f[i + 1]))
             put(i + 1, jnp.where(isf, keep * f[i + 1] + (e - o), f[i]))
 
+        if ions_out is None:
+            continue
         fl = fluid[x + 1, mid, :]
         near = [
             ((x + 2, mid), (x, mid)),
@@ -173,6 +191,112 @@
         out[i, 0] = plane
 
 
+def split(x):
+    hi = x.astype(jnp.bfloat16)
+    return hi, (x - hi.astype(jnp.float32)).astype(jnp.bfloat16)
+
+
+def dot3(a, b):
+    d = lambda x, y: jnp.dot(x, y, preferred_element_type=jnp.float32)
+    return d(a[0], b[0]) + (d(a[0], b[1]) + d(a[1], b[0]))
+
+
+def swap_groups(planes, group):
+    planes = list(planes)
+    lane = lax.broadcasted_iota(jnp.int32, planes[0].shape, 1) // group
+    bit = 1
+    while bit < len(planes):
+        low = lane & bit == 0
+        for i in range(len(planes)):
+            if i & bit:
+                continue
+            a, b = planes[i], planes[i | bit]
+            planes[i] = jnp.where(low, a, shifted(b, bit * group, 1))
+            planes[i | bit] = jnp.where(low, shifted(a, -bit * group, 1), b)
+        bit *= 2
+    return planes
+
+
+def depth_forward_kernel(ion, mask, shi, slo, out):
+    length, wid, depth = mask.shape
+    groups = length
+    charge = jnp.where(mask[...] == 0, ion[0] - ion[1], WALL_CHARGE)
+    t = dot3(split(charge.reshape(length * wid, depth)), (shi[...], slo[...]))
+    for j in range(depth // 128):
+        planes = [t[x * wid : (x + 1) * wid, j * 128 : (j + 1) * 128] for x in range(length)]
+        for g, plane in enumerate(swap_groups(planes, 128 // groups)):
+            out[j * groups + g] = plane
+
+
+def depth_back_kernel(t, shi, slo, out):
+    length, wid, depth = out.shape
+    groups = length
+    halves = []
+    for j in range(depth // 128):
+        planes = swap_groups([t[j * groups + g] for g in range(groups)], 128 // groups)
+        halves.append(jnp.concatenate(planes, axis=0))
+    v = jnp.concatenate(halves, axis=1)
+    out[...] = dot3(split(v), (shi[...], slo[...])).reshape(length, wid, depth)
+
+
+def plane_kernel(t, shi, slo, hhi, hlo, scale, out):
+    gx = t.shape[0]
+    sines, waves = (shi[...], slo[...]), (hhi[...], hlo[...])
+    v = jnp.concatenate([t[g] for g in range(gx)], axis=1)
+    v = dot3(sines, split(v))
+    v = dot3(split(v), waves)
+    v = v / scale[...]
+    v = dot3(split(v), waves)
+    v = dot3(sines, split(v))
+    for g in range(gx):
+        out[g] = v[:, g * 128 : (g + 1) * 128]
+
+
+def halves(table):
+    hi = table.astype(jnp.bfloat16)
+    return hi, (table - hi.astype(np.float32)).astype(jnp.bfloat16)
+
+
+def wall(first, number, total):
+    m = (jnp.arange(number, dtype=jnp.int32) + first + 1).astype(jnp.float32)
+    return 2.0 - 2.0 * jnp.cos(m * (math.pi / (total + 1)))
+
+
+def solve_packed(ions, mask):
+    length, wid, depth = mask.shape
+    gx, gy = lax.axis_size("gx"), lax.axis_size("gy")
+    parts = gx * gy
+    modes = depth // parts
+    full_len, full_wid = length * gx, wid * gy
+    sz, sy, hx = sine_table(depth), sine_table(full_wid), hartley_table(full_len)
+    waves = np.kron(hx, np.eye(modes, dtype=np.float32))
+    params = pltpu.CompilerParams(vmem_limit_bytes=48 << 20)
+    chunk = jax.ShapeDtypeStruct((parts, wid, 128), jnp.float32)
+    t = pl.pallas_call(depth_forward_kernel, out_shape=chunk, compiler_params=params)(
+        ions, mask, *halves(sz)
+    )
+    t = lax.all_to_all(t, ("gx", "gy"), split_axis=0, concat_axis=0, tiled=True)
+    me = lax.axis_index("gx") * gy + lax.axis_index("gy")
+    ex = (2.0 - 2.0 * np.cos(np.arange(full_len) * (2.0 * math.pi / full_len))).astype(np.float32)
+    along = SCREENING + (ex[:, None] + wall(me * modes, modes, depth)[None, :]).reshape(1, -1)
+    scale = (along + wall(0, full_wid, full_wid)[:, None]) * (
+        (full_wid + 1) * (depth + 1) / 4.0
+    )
+    t = pl.pallas_call(
+        plane_kernel,
+        out_shape=jax.ShapeDtypeStruct((gx, full_wid, 128), jnp.float32),
+        compiler_params=params,
+    )(t.reshape(gx, full_wid, 128), *halves(sy), *halves(waves), scale)
+    t = lax.all_to_all(
+        t.reshape(parts, wid, 128), ("gx", "gy"), split_axis=0, concat_axis=0, tiled=True
+    )
+    return pl.pallas_call(
+        depth_back_kernel,
+        out_shape=jax.ShapeDtypeStruct((length, wid, depth), jnp.float32),
+        compiler_params=params,
+    )(t, *halves(sz))
+
+
 def solve(charge):
     length, wid, depth = charge.shape
     gx, gy = lax.axis_size("gx"), lax.axis_size("gy")
@@ -189,10 +313,6 @@
     t = jnp.einsum("kx,nxm->nkm", hx, t, precision=PRECISE)
     me = lax.axis_index("gx") * gy + lax.axis_index("gy")
 
-    def wall(first, number, total):
-        m = (jnp.arange(number, dtype=jnp.int32) + first + 1).astype(jnp.float32)
-        return 2.0 - 2.0 * jnp.cos(m * (math.pi / (total + 1)))
-
     ex = (2.0 - 2.0 * np.cos(np.arange(full_len) * (2.0 * math.pi / full_len))).astype(np.float32)
     denom = (
         SCREENING
@@ -229,7 +349,8 @@
     fluid = (mask == 0).astype(jnp.float32)
     charge = fluid * (ions[0] - ions[1]) + (1.0 - fluid) * WALL_CHARGE
     ionic = beside(jnp.concatenate([ions, fluid[None]], axis=0), 1.0, 1.0)
-    potential = solve(charge)
+    packed = length * (depth // (lax.axis_size("gx") * lax.axis_size("gy"))) == 128
+    potential = solve_packed(ions, mask) if packed else solve(charge)
     pot = beside(
         potential,
         (ygo != 0).astype(jnp.float32),
@@ -240,45 +361,45 @@
     whole = pl.BlockSpec(memory_space=pltpu.VMEM)
     shape = lambda n: jax.ShapeDtypeStruct((n, length, wid, depth), jnp.float32)
     cells = length * wid * depth
-    p0, pp, pm, ions_out = pl.pallas_call(
+    face_p, face_m = pl.pallas_call(
+        functools.partial(faces_kernel, length),
+        grid=(2,),
+        in_specs=[block(19, lambda x: x * (length - 1)), whole, whole, whole],
+        out_specs=[whole, whole],
+        out_shape=[jax.ShapeDtypeStruct((5, 1, wid, depth), jnp.float32)] * 2,
+        compiler_params=pltpu.CompilerParams(vmem_limit_bytes=32 << 20),
+        cost_estimate=pl.CostEstimate(
+            flops=800 * wid * depth, bytes_accessed=4 * 48 * wid * depth, transcendentals=0
+        ),
+    )(populations, ionic[:2], ionic[2], pot)
+    hl = up(face_p[:, 0], "gx")
+    hr = down(face_m[:, 0], "gx")
+    edge = jax.ShapeDtypeStruct((5, length, depth), jnp.float32)
+    p0, pp, pm, ions_out, top, bottom = pl.pallas_call(
         collide_kernel,
         grid=(length,),
         in_specs=[block(19, same), whole, whole, whole],
-        out_specs=[block(9, same), block(5, same), block(5, same), block(2, same)],
-        out_shape=[shape(9), shape(5), shape(5), shape(2)],
+        out_specs=[block(9, same), block(5, same), block(5, same), block(2, same), whole, whole],
+        out_shape=[shape(9), shape(5), shape(5), shape(2), edge, edge],
         compiler_params=pltpu.CompilerParams(vmem_limit_bytes=32 << 20),
         cost_estimate=pl.CostEstimate(
             flops=500 * cells, bytes_accessed=4 * 44 * cells, transcendentals=0
         ),
     )(populations, ionic[:2], ionic[2], pot)
 
-    hl = up(pp[:, length - 1], "gx")
-    hr = down(pm[:, 0], "gx")
-
-    def row(i, y):
-        if i in XP:
-            return pp[XP.index(i), :, y]
-        if i in XM:
-            return pm[XM.index(i), :, y]
-        return p0[X0.index(i), :, y]
-
-    def moved(i, rows, beside_left, beside_right):
-        if i in XP:
-            return jnp.concatenate([beside_left, rows[:-1]], axis=0)
-        if i in XM:
-            return jnp.concatenate([rows[1:], beside_right], axis=0)
-        return rows
-
-    def rows_of(group, y):
+    def moved(rows, group, y):
         out = []
-        for i in group:
-            a = hl[XP.index(i), y][None] if i in XP else None
-            b = hr[XM.index(i), y][None] if i in XM else None
-            out.append(moved(i, row(i, y), a, b))
+        for k, i in enumerate(group):
+            r = rows[k]
+            if i in XP:
+                r = jnp.concatenate([hl[XP.index(i), y][None], r[:-1]], axis=0)
+            elif i in XM:
+                r = jnp.concatenate([r[1:], hr[XM.index(i), y][None]], axis=0)
+            out.append(r)
         return jnp.stack(out)
 
-    hb = up(rows_of(YP, wid - 1), "gy")
-    ht = down(rows_of(YM, 0), "gy")
+    hb = up(moved(top, YP, wid - 1), "gy")
+    ht = down(moved(bottom, YM, 0), "gy")
     populations_out = pl.pallas_call(
         stream_kernel,
         grid=(length,),

time: 114 us -> 113 us (level)
  local copies, waits for them, and re-layouts: 20.3 us -> 11 us
  Pallas kernels: 24 us -> 32.9 us
  matrix products: 3.43 us -> 0 us
  waiting for transfers between devices: 36.6 us -> 39.2 us
    reshape x5 -> x0, local copies, waits for them, and re-layouts: 7.91 us -> none  [the longest x1 3.03 us: solve(): t = t.reshape(parts, modes, length * wid)]
    pallas_call x0 -> x4, Pallas kernels: none -> 6.61 us  [the longest x1 2.49 us: solve_packed(): pl.pallas_call(plane_kernel, out_shape=jax.ShapeDtypeStruct((gx, full_wid...]
    pallas_call x3 -> x0, local copies, waits for them, and re-layouts: 5.78 us -> none  [body(): pl.pallas_call(collide_kernel, grid=(length,), in_specs=[block(19, same),...]
    unnamed x16 -> x24, local copies, waits for them, and re-layouts: 3.87 us -> 8.96 us
    dot_general x6 -> x0, matrix products: 3.43 us -> none  [the longest x1 1.22 us: solve(): jnp.einsum('nz,pz->np', sz, charge.reshape(length * wid, depth), precisio...]
    ppermute x6, waiting for transfers between devices: 2.17 us -> 4.99 us  [down(): return lax.ppermute(x, axis, [((i + 1) % n, i) for i in range(n)])]
    transpose x1 -> x0, local copies, waits for them, and re-layouts: 2.54 us -> none  [solve(): t = t.reshape(gx, gy, modes, length, wid).transpose(2, 0, 3, 1, 4)]
    pallas_call x1, Pallas kernels: 15.5 us -> 17.8 us  [body(): pl.pallas_call(collide_kernel, grid=(length,), in_specs=[block(19, same),...]
  transfers between devices with their start and end apart: 14 -> 14, of which waited for: 7 -> 8; matrix products, arithmetic and copies ran while one was open for 3% -> 2% of each run, Pallas kernels for 0% -> 0%
where the time goes in v1:
time: 113 us; the launch traced here: 112 us
  waiting for transfers between devices  39.2 us (35%)
  Pallas kernels  32.9 us (29%)
  starting transfers between devices  26.6 us (24%)
  local copies, waits for them, and re-layouts  11 us (10%)
  other arithmetic  1.87 us (2%)
    pallas_call x1, Pallas kernels, body(): pl.pallas_call(collide_kernel, grid=(length,), in_specs=[block(19, same),...  17.8 us
    all_to_all x1, waiting for transfers between devices, solve_packed(): t = lax.all_to_all(t, ('gx', 'gy'), split_axis=0, concat_axis=0, tiled=True)  15.9 us
    ppermute x6, waiting for transfers between devices, up(): return lax.ppermute(x, axis, [(i, (i + 1) % n) for i in range(n)])  15.6 us
    ppermute x6, starting transfers between devices, down(): return lax.ppermute(x, axis, [((i + 1) % n, i) for i in range(n)])  14.7 us
    unnamed x24, local copies, waits for them, and re-layouts  8.96 us
    pallas_call x1, Pallas kernels, body(): pl.pallas_call(stream_kernel, grid=(length,), in_specs=[block(9, same), b...  8.51 us
    all_to_all x1, starting transfers between devices, solve_packed(): t = lax.all_to_all(t, ('gx', 'gy'), split_axis=0, concat_axis=0, tiled=True)  7.3 us
    ppermute x6, waiting for transfers between devices, down(): return lax.ppermute(x, axis, [((i + 1) % n, i) for i in range(n)])  4.99 us
  transfers between devices with their start and end apart: 14, of which 8 were waited for; matrix products, arithmetic and copies ran while one was open for 2% of the time, Pallas kernels for 0%

profile of v1, /device:TPU:0, one launch (start us, length us, event | category | flops | bytes accessed | tf_op | source)
XLA Modules:
  0.0 112.5 jit_solution(17206113072175954743)
XLA Ops:
  0.7 1.2 %copy-done.1 = f32[2,16,32,256]{3,2,1,0:T(8,128)S(1)} copy-done((f32[2,16,32,256]{3,2,1,0:T(8,128)S(1)}, f32[2,16,32,256]{3,2,1,0:T(8,128)}, u32[]{:S(2)}) %copy-start.1) | copy-done | bytes 1048600
  4.7 1.6 %shard_map.139 = f32[32,32,128]{2,1,0:T(8,128)} custom-call(f32[2,16,32,256]{3,2,1,0:T(8,128)S(1)} %copy-done.1, s32[16,32,256]{2,1,0:T(8,128)S(1)} %copy-done.3, bf16[256,256]{1,0:T(8,128)(2,1)S(1)} %copy-done.7, bf16[256,256]{1,0:T(8,128)(2,1)S(1)} %copy-done.5), custom_call_target="tpu_custom_call" | custom-call | tf_op jit(solution)/shard_map/pallas_call | solution.py:275
  6.4 7.3 %all-to-all-start = ((f32[32,32,128]{2,1,0:T(8,128)}), f32[32,32,128]{2,1,0:T(8,128)S(1)}, u32[]{:S(2)}, u32[]{:S(2)}) async-start(f32[32,32,128]{2,1,0:T(8,128)} %shard_map.139), calls=%async_computation | async-start | bytes 1048576 | tf_op jit(solution)/shard_map/all_to_all | solution.py:278
  14.1 15.9 %all-to-all-done = f32[32,32,128]{2,1,0:T(8,128)S(1)} async-done(((f32[32,32,128]{2,1,0:T(8,128)}), f32[32,32,128]{2,1,0:T(8,128)S(1)}, u32[]{:S(2)}, u32[]{:S(2)}) %all-to-all-start) | async-done | bytes 524320 | tf_op jit(solution)/shard_map/all_to_all | solution.py:278
  31.1 2.5 %shard_map.140 = f32[4,256,128]{2,1,0:T(8,128)} custom-call(f32[4,256,128]{2,1,0:T(8,128)S(1)} %bitcast.36, bf16[256,256]{1,0:T(8,128)(2,1)S(1)} %copy-done.8, bf16[256,256]{1,0:T(8,128)(2,1)S(1)} %copy-done.6, bf16[512,512]{1,0:T(8,128)(2,1)S(1)} %copy-done.10, bf16[512,512]{1,0:T(8,128)(2,1)S(1)} %copy-done.9, f32[256,512]{1,0:T(8,128)S(1)} %add_multiply_fusion.scale), custom_call_target="tpu_custom_call" | custom-call | tf_op jit(solution)/shard_map/pallas_call | solution.py:285
  33.6 2.6 %all-to-all-start.1 = ((f32[32,32,128]{2,1,0:T(8,128)}), f32[32,32,128]{2,1,0:T(8,128)S(1)}, u32[]{:S(2)}, u32[]{:S(2)}) async-start(f32[32,32,128]{2,1,0:T(8,128)} %bitcast.3), calls=%async_computation.1 | async-start | bytes 1048576 | tf_op jit(solution)/shard_map/all_to_all | solution.py:290
  36.3 1.7 %collective-permute-start = (f32[3,1,32,256]{3,2,1,0:T(8,128)S(1)}, f32[3,1,32,256]{3,2,1,0:T(8,128)S(1)}, u32[]{:S(2)}, u32[]{:S(2)}) collective-permute-start(f32[3,1,32,256]{3,2,1,0:T(8,128)S(1)} %get-tuple-element.21), channel_id=1, source_target_pairs={{0,8},{8,16},{16,24},{24,0},{1,9},{9,17},{17,25},{25,1},{2,10},{10... | collective-permute-start | bytes 294920 | tf_op jit(solution)/shard_map/ppermute | solution.py:44
  38.0 1.3 %collective-permute-start.3 = (f32[3,1,32,256]{3,2,1,0:T(8,128)S(1)}, f32[3,1,32,256]{3,2,1,0:T(8,128)S(1)}, u32[]{:S(2)}, u32[]{:S(2)}) collective-permute-start(f32[3,1,32,256]{3,2,1,0:T(8,128)S(1)} %get-tuple-element.22), channel_id=1, source_target_pairs={{8,0},{16,8},{24,16},{0,24},{9,1},{17,9},{25,17},{1,25},{10,2},{18... | collective-permute-start | bytes 294920 | tf_op jit(solution)/shard_map/ppermute | solution.py:49
  39.4 3.5 %collective-permute-start.2 = (f32[3,16,1,256]{3,2,1,0:T(1,128)S(1)}, f32[3,16,1,256]{3,2,1,0:T(1,128)S(1)}, u32[]{:S(2)}, u32[]{:S(2)}) collective-permute-start(f32[3,16,1,256]{3,2,1,0:T(1,128)S(1)} %get-tuple-element.20), channel_id=1, source_target_pairs={{1,0},{2,1},{3,2},{4,3},{5,4},{6,5},{7,6},{0,7},{9,8},{10,9},{11,1... | collective-permute-start | bytes 147464 | tf_op jit(solution)/shard_map/ppermute | solution.py:49
  43.0 7.0 %collective-permute-done.1 = f32[3,16,1,256]{3,2,1,0:T(1,128)S(1)} collective-permute-done((f32[3,16,1,256]{3,2,1,0:T(1,128)S(1)}, f32[3,16,1,256]{3,2,1,0:T(1,128)S(1)}, u32[]{:S(2)}, u32[]{:S(2)}) %collective-permute-start.1) | collective-permute-done | bytes 49184 | tf_op jit(solution)/shard_map/ppermute | solution.py:44
  50.4 2.7 %all-to-all-done.1.t = f32[32,32,128]{2,1,0:T(8,128)S(1)} async-done(((f32[32,32,128]{2,1,0:T(8,128)}), f32[32,32,128]{2,1,0:T(8,128)S(1)}, u32[]{:S(2)}, u32[]{:S(2)}) %all-to-all-start.1) | async-done | bytes 524320 | tf_op jit(solution)/shard_map/all_to_all | solution.py:290
  53.1 1.6 %shard_map.141 = f32[16,32,256]{2,1,0:T(8,128)} custom-call(f32[32,32,128]{2,1,0:T(8,128)S(1)} %all-to-all-done.1.t, bf16[256,256]{1,0:T(8,128)(2,1)S(1)} %copy-done.8, bf16[256,256]{1,0:T(8,128)(2,1)S(1)} %copy-done.6), custom_call_target="tpu_custom_call" | custom-call | tf_op jit(solution)/shard_map/pallas_call | solution.py:293
  56.6 3.5 %collective-permute-start.6 = (f32[16,1,256]{2,1,0:T(1,128)S(1)}, f32[16,1,256]{2,1,0:T(1,128)S(1)}, u32[]{:S(2)}, u32[]{:S(2)}) collective-permute-start(f32[16,1,256]{2,1,0:T(1,128)S(1)} %get-tuple-element.24), channel_id=1, source_target_pairs={{1,0},{2,1},{3,2},{4,3},{5,4},{6,5},{7,6},{0,7},{9,8},{10,9},{11,1... | collective-permute-start | bytes 49160 | tf_op jit(solution)/shard_map/ppermute | solution.py:49
  60.1 2.9 %collective-permute-start.7 = (f32[1,32,256]{2,1,0:T(8,128)S(1)}, f32[1,32,256]{2,1,0:T(8,128)S(1)}, u32[]{:S(2)}, u32[]{:S(2)}) collective-permute-start(f32[1,32,256]{2,1,0:T(8,128)S(1)} %get-tuple-element.26), channel_id=1, source_target_pairs={{8,0},{16,8},{24,16},{0,24},{9,1},{17,9},{25,17},{1,25},{10,2},{18... | collective-permute-start | bytes 98312 | tf_op jit(solution)/shard_map/ppermute | solution.py:49
  63.0 1.9 %collective-permute-done.4 = f32[1,32,256]{2,1,0:T(8,128)S(1)} collective-permute-done((f32[1,32,256]{2,1,0:T(8,128)S(1)}, f32[1,32,256]{2,1,0:T(8,128)S(1)}, u32[]{:S(2)}, u32[]{:S(2)}) %collective-permute-start.4) | collective-permute-done | bytes 32800 | tf_op jit(solution)/shard_map/ppermute | solution.py:44
  64.9 1.1 select_maximum_fusion.2.pot
  66.0 3.8 %copy-done = f32[19,16,32,256]{3,2,1,0:T(8,128)S(1)} copy-done((f32[19,16,32,256]{3,2,1,0:T(8,128)S(1)}, f32[19,16,32,256]{3,2,1,0:T(8,128)}, u32[]{:S(2)}) %copy-start) | copy-done | bytes 9961496
  70.7 17.8 %shard_map.142 = (f32[9,16,32,256]{3,2,1,0:T(8,128)S(1)}, f32[5,16,32,256]{3,2,1,0:T(8,128)S(1)}, f32[5,16,32,256]{3,2,1,0:T(8,128)S(1)}, f32[2,16,32,256]{3,2,1...) custom-call(f32[19,16,32,256]{3,2,1,0:T(8,128)} %pop.3, f32[2,18,34,256]{3,2,1,0:T(8,128)S(1)} %slice.118.ion, ...), custom_call_target="tpu_custom_call" | custom-call | flops 65536000 | bytes 23068672 | tf_op jit(solution)/shard_map/pallas_call | solution.py:378
  88.5 3.0 %collective-permute-start.9 = (f32[5,32,256]{2,1,0:T(8,128)S(1)}, f32[5,32,256]{2,1,0:T(8,128)S(1)}, u32[]{:S(2)}, u32[]{:S(2)}) collective-permute-start(f32[5,32,256]{2,1,0:T(8,128)S(1)} %bitcast.38), channel_id=1, source_target_pairs={{8,0},{16,8},{24,16},{0,24},{9,1},{17,9},{25,17},{1,25},{10,2},{18... | collective-permute-start | bytes 491528 | tf_op jit(solution)/shard_map/ppermute | solution.py:49
  91.5 2.8 %collective-permute-done.9.hr = f32[5,32,256]{2,1,0:T(8,128)S(1)} collective-permute-done((f32[5,32,256]{2,1,0:T(8,128)S(1)}, f32[5,32,256]{2,1,0:T(8,128)S(1)}, u32[]{:S(2)}, u32[]{:S(2)}) %collective-permute-start.9) | collective-permute-done | bytes 163872 | tf_op jit(solution)/shard_map/ppermute | solution.py:49
  94.4 3.4 %collective-permute-done.8.hl = f32[5,32,256]{2,1,0:T(8,128)S(1)} collective-permute-done((f32[5,32,256]{2,1,0:T(8,128)S(1)}, f32[5,32,256]{2,1,0:T(8,128)S(1)}, u32[]{:S(2)}, u32[]{:S(2)}) %collective-permute-start.8) | collective-permute-done | bytes 163872 | tf_op jit(solution)/shard_map/ppermute | solution.py:44
  98.4 2.2 %collective-permute-done.11.ht = f32[5,16,256]{2,1,0:T(8,128)S(1)} collective-permute-done((f32[5,16,256]{2,1,0:T(8,128)S(1)}, f32[5,16,256]{2,1,0:T(8,128)S(1)}, u32[]{:S(2)}, u32[]{:S(2)}) %collective-permute-start.11) | collective-permute-done | bytes 81952 | tf_op jit(solution)/shard_map/ppermute | solution.py:49
  100.6 3.4 %collective-permute-done.10.hb = f32[5,16,256]{2,1,0:T(8,128)S(1)} collective-permute-done((f32[5,16,256]{2,1,0:T(8,128)S(1)}, f32[5,16,256]{2,1,0:T(8,128)S(1)}, u32[]{:S(2)}, u32[]{:S(2)}) %collective-permute-start.10) | collective-permute-done | bytes 81952 | tf_op jit(solution)/shard_map/ppermute | solution.py:44
  104.0 8.5 %shard_map.144 = f32[19,16,32,256]{3,2,1,0:T(8,128)} custom-call(f32[9,16,32,256]{3,2,1,0:T(8,128)S(1)} %get-tuple-element.11.p0, f32[5,16,32,256]{3,2,1,0:T(8,128)S(1)} %get-tuple-element.12.pp, f32[5,16,32,256]{3,2,1,0:T(8,128)S(1)} %get-tuple-element.13.pm, f32[5,32,256]{2,1,0:T(8,128)S(1)} %collective-permute-done.8.hl, ...), custom_call_target="tpu_custom_call" | custom-call | flops 2621440 | bytes 19922944 | tf_op jit(solution)/shard_map/pallas_call | solution.py:403
  (62 shorter events, 8.3 us)
Async XLA Ops:
  0.6 13.1 %copy-start.11 = (f32[64]{0:T(128)S(1)}, f32[64]{0:T(128)}, u32[]{:S(2)}) copy-start(f32[64]{0:T(128)} %constant.53) | copy-start | bytes 772
  0.6 1.2 %copy-start.1 = (f32[2,16,32,256]{3,2,1,0:T(8,128)S(1)}, f32[2,16,32,256]{3,2,1,0:T(8,128)}, u32[]{:S(2)}) copy-start(f32[2,16,32,256]{3,2,1,0:T(8,128)} %ion.1) | copy-start | bytes 3145732
  1.9 1.0 copy-start.3
  4.7 25.3 %copy-start.6 = (bf16[256,256]{1,0:T(8,128)(2,1)S(1)}, bf16[256,256]{1,0:T(8,128)(2,1)}, u32[]{:S(2)}) copy-start(bf16[256,256]{1,0:T(8,128)(2,1)} %constant.41.clone.slo) | copy-start | bytes 393220
  4.7 25.3 %copy-start.8 = (bf16[256,256]{1,0:T(8,128)(2,1)S(1)}, bf16[256,256]{1,0:T(8,128)(2,1)}, u32[]{:S(2)}) copy-start(bf16[256,256]{1,0:T(8,128)(2,1)} %constant.40.clone.shi) | copy-start | bytes 393220
  4.7 25.3 %copy-start.9 = (bf16[512,512]{1,0:T(8,128)(2,1)S(1)}, bf16[512,512]{1,0:T(8,128)(2,1)}, u32[]{:S(2)}) copy-start(bf16[512,512]{1,0:T(8,128)(2,1)} %constant.44.clone.hlo) | copy-start | bytes 1572868
  6.4 23.7 %all-to-all-start = ((f32[32,32,128]{2,1,0:T(8,128)}), f32[32,32,128]{2,1,0:T(8,128)S(1)}, u32[]{:S(2)}, u32[]{:S(2)}) async-start(f32[32,32,128]{2,1,0:T(8,128)} %shard_map.139), calls=%async_computation | async-start | bytes 1048576 | tf_op jit(solution)/shard_map/all_to_all | solution.py:278
  14.0 22.2 %copy-start.4 = (s32[16,32,256]{2,1,0:T(8,128)S(1)}, s32[16,32,256]{2,1,0:T(8,128)}, u32[]{:S(2)}) copy-start(s32[16,32,256]{2,1,0:T(8,128)} %mask.1) | copy-start | bytes 1572868
  30.0 1.0 copy-start.10
  31.1 5.2 %copy-start.2 = (f32[2,16,32,256]{3,2,1,0:T(8,128)S(1)}, f32[2,16,32,256]{3,2,1,0:T(8,128)}, u32[]{:S(2)}) copy-start(f32[2,16,32,256]{3,2,1,0:T(8,128)} %ion.1) | copy-start | bytes 3145732
  33.6 19.5 %all-to-all-start.1 = ((f32[32,32,128]{2,1,0:T(8,128)}), f32[32,32,128]{2,1,0:T(8,128)S(1)}, u32[]{:S(2)}, u32[]{:S(2)}) async-start(f32[32,32,128]{2,1,0:T(8,128)} %bitcast.3), calls=%async_computation.1 | async-start | bytes 1048576 | tf_op jit(solution)/shard_map/all_to_all | solution.py:290
  36.3 13.6 %collective-permute-start = (f32[3,1,32,256]{3,2,1,0:T(8,128)S(1)}, f32[3,1,32,256]{3,2,1,0:T(8,128)S(1)}, u32[]{:S(2)}, u32[]{:S(2)}) collective-permute-start(f32[3,1,32,256]{3,2,1,0:T(8,128)S(1)} %get-tuple-element.21), channel_id=1, source_target_pairs={{0,8},{8,16},{16,24},{24,0},{1,9},{9,17},{17,25},{25,1},{2,10},{10... | collective-permute-start | bytes 294920 | tf_op jit(solution)/shard_map/ppermute | solution.py:44
  38.0 11.9 %collective-permute-start.3 = (f32[3,1,32,256]{3,2,1,0:T(8,128)S(1)}, f32[3,1,32,256]{3,2,1,0:T(8,128)S(1)}, u32[]{:S(2)}, u32[]{:S(2)}) collective-permute-start(f32[3,1,32,256]{3,2,1,0:T(8,128)S(1)} %get-tuple-element.22), channel_id=1, source_target_pairs={{8,0},{16,8},{24,16},{0,24},{9,1},{17,9},{25,17},{1,25},{10,2},{18... | collective-permute-start | bytes 294920 | tf_op jit(solution)/shard_map/ppermute | solution.py:49
  39.4 10.6 %collective-permute-start.1 = (f32[3,16,1,256]{3,2,1,0:T(1,128)S(1)}, f32[3,16,1,256]{3,2,1,0:T(1,128)S(1)}, u32[]{:S(2)}, u32[]{:S(2)}) collective-permute-start(f32[3,16,1,256]{3,2,1,0:T(1,128)S(1)} %get-tuple-element.19), channel_id=1, source_target_pairs={{0,1},{1,2},{2,3},{3,4},{4,5},{5,6},{6,7},{7,0},{8,9},{9,10},{10,1... | collective-permute-start | bytes 147464 | tf_op jit(solution)/shard_map/ppermute | solution.py:44
  39.4 10.5 %collective-permute-start.2 = (f32[3,16,1,256]{3,2,1,0:T(1,128)S(1)}, f32[3,16,1,256]{3,2,1,0:T(1,128)S(1)}, u32[]{:S(2)}, u32[]{:S(2)}) collective-permute-start(f32[3,16,1,256]{3,2,1,0:T(1,128)S(1)} %get-tuple-element.20), channel_id=1, source_target_pairs={{1,0},{2,1},{3,2},{4,3},{5,4},{6,5},{7,6},{0,7},{9,8},{10,9},{11,1... | collective-permute-start | bytes 147464 | tf_op jit(solution)/shard_map/ppermute | solution.py:49
  55.7 7.3 %collective-permute-start.5 = (f32[16,1,256]{2,1,0:T(1,128)S(1)}, f32[16,1,256]{2,1,0:T(1,128)S(1)}, u32[]{:S(2)}, u32[]{:S(2)}) collective-permute-start(f32[16,1,256]{2,1,0:T(1,128)S(1)} %get-tuple-element.23), channel_id=1, source_target_pairs={{0,1},{1,2},{2,3},{3,4},{4,5},{5,6},{6,7},{7,0},{8,9},{9,10},{10,1... | collective-permute-start | bytes 49160 | tf_op jit(solution)/shard_map/ppermute | solution.py:44
  56.6 6.5 %collective-permute-start.6 = (f32[16,1,256]{2,1,0:T(1,128)S(1)}, f32[16,1,256]{2,1,0:T(1,128)S(1)}, u32[]{:S(2)}, u32[]{:S(2)}) collective-permute-start(f32[16,1,256]{2,1,0:T(1,128)S(1)} %get-tuple-element.24), channel_id=1, source_target_pairs={{1,0},{2,1},{3,2},{4,3},{5,4},{6,5},{7,6},{0,7},{9,8},{10,9},{11,1... | collective-permute-start | bytes 49160 | tf_op jit(solution)/shard_map/ppermute | solution.py:49
  60.1 4.8 %collective-permute-start.4 = (f32[1,32,256]{2,1,0:T(8,128)S(1)}, f32[1,32,256]{2,1,0:T(8,128)S(1)}, u32[]{:S(2)}, u32[]{:S(2)}) collective-permute-start(f32[1,32,256]{2,1,0:T(8,128)S(1)} %get-tuple-element.25), channel_id=1, source_target_pairs={{0,8},{8,16},{16,24},{24,0},{1,9},{9,17},{17,25},{25,1},{2,10},{10... | collective-permute-start | bytes 98312 | tf_op jit(solution)/shard_map/ppermute | solution.py:44
  60.1 4.8 %collective-permute-start.7 = (f32[1,32,256]{2,1,0:T(8,128)S(1)}, f32[1,32,256]{2,1,0:T(8,128)S(1)}, u32[]{:S(2)}, u32[]{:S(2)}) collective-permute-start(f32[1,32,256]{2,1,0:T(8,128)S(1)} %get-tuple-element.26), channel_id=1, source_target_pairs={{8,0},{16,8},{24,16},{0,24},{9,1},{17,9},{25,17},{1,25},{10,2},{18... | collective-permute-start | bytes 98312 | tf_op jit(solution)/shard_map/ppermute | solution.py:49
  66.0 3.8 %copy-start = (f32[19,16,32,256]{3,2,1,0:T(8,128)S(1)}, f32[19,16,32,256]{3,2,1,0:T(8,128)}, u32[]{:S(2)}) copy-start(f32[19,16,32,256]{3,2,1,0:T(8,128)} %pop.3) | copy-start | bytes 29884420
  88.5 5.8 %collective-permute-start.9 = (f32[5,32,256]{2,1,0:T(8,128)S(1)}, f32[5,32,256]{2,1,0:T(8,128)S(1)}, u32[]{:S(2)}, u32[]{:S(2)}) collective-permute-start(f32[5,32,256]{2,1,0:T(8,128)S(1)} %bitcast.38), channel_id=1, source_target_pairs={{8,0},{16,8},{24,16},{0,24},{9,1},{17,9},{25,17},{1,25},{10,2},{18... | collective-permute-start | bytes 491528 | tf_op jit(solution)/shard_map/ppermute | solution.py:49
  91.5 6.2 %collective-permute-start.8 = (f32[5,32,256]{2,1,0:T(8,128)S(1)}, f32[5,32,256]{2,1,0:T(8,128)S(1)}, u32[]{:S(2)}, u32[]{:S(2)}) collective-permute-start(f32[5,32,256]{2,1,0:T(8,128)S(1)} %bitcast.37), channel_id=1, source_target_pairs={{0,8},{8,16},{16,24},{24,0},{1,9},{9,17},{17,25},{25,1},{2,10},{10... | collective-permute-start | bytes 491528 | tf_op jit(solution)/shard_map/ppermute | solution.py:44
  97.8 2.8 %collective-permute-start.11 = (f32[5,16,256]{2,1,0:T(8,128)S(1)}, f32[5,16,256]{2,1,0:T(8,128)S(1)}, u32[]{:S(2)}, u32[]{:S(2)}) collective-permute-start(f32[5,16,256]{2,1,0:T(8,128)S(1)} %pad_maximum_fusion.3), channel_id=1, source_target_pairs={{1,0},{2,1},{3,2},{4,3},{5,4},{6,5},{7,6},{0,7},{9,8},{10,9},{11,1... | collective-permute-start | bytes 245768 | tf_op jit(solution)/shard_map/ppermute | solution.py:49
  98.2 5.7 %collective-permute-start.10 = (f32[5,16,256]{2,1,0:T(8,128)S(1)}, f32[5,16,256]{2,1,0:T(8,128)S(1)}, u32[]{:S(2)}, u32[]{:S(2)}) collective-permute-start(f32[5,16,256]{2,1,0:T(8,128)S(1)} %pad_maximum_fusion.2), channel_id=1, source_target_pairs={{0,1},{1,2},{2,3},{3,4},{4,5},{5,6},{6,7},{7,0},{8,9},{9,10},{10,1... | collective-permute-start | bytes 245768 | tf_op jit(solution)/shard_map/ppermute | solution.py:44
  (2 other events, 1.8 us)

commit v2 on v1

--- a/solution.py
+++ b/solution.py
@@ -217,18 +217,18 @@
     return planes
 
 
-def depth_forward_kernel(ion, mask, shi, slo, out):
+def depth_forward_kernel(ion, mask, s, out):
     length, wid, depth = mask.shape
     groups = length
     charge = jnp.where(mask[...] == 0, ion[0] - ion[1], WALL_CHARGE)
-    t = dot3(split(charge.reshape(length * wid, depth)), (shi[...], slo[...]))
+    t = dot3(split(charge.reshape(length * wid, depth)), (s[0], s[1]))
     for j in range(depth // 128):
         planes = [t[x * wid : (x + 1) * wid, j * 128 : (j + 1) * 128] for x in range(length)]
         for g, plane in enumerate(swap_groups(planes, 128 // groups)):
             out[j * groups + g] = plane
 
 
-def depth_back_kernel(t, shi, slo, out):
+def depth_back_kernel(t, s, out):
     length, wid, depth = out.shape
     groups = length
     halves = []
@@ -236,12 +236,12 @@
         planes = swap_groups([t[j * groups + g] for g in range(groups)], 128 // groups)
         halves.append(jnp.concatenate(planes, axis=0))
     v = jnp.concatenate(halves, axis=1)
-    out[...] = dot3(split(v), (shi[...], slo[...])).reshape(length, wid, depth)
-
-
-def plane_kernel(t, shi, slo, hhi, hlo, scale, out):
+    out[...] = dot3(split(v), (s[0], s[1])).reshape(length, wid, depth)
+
+
+def plane_kernel(t, s, h, scale, out):
     gx = t.shape[0]
-    sines, waves = (shi[...], slo[...]), (hhi[...], hlo[...])
+    sines, waves = (s[0], s[1]), (h[0], h[1])
     v = jnp.concatenate([t[g] for g in range(gx)], axis=1)
     v = dot3(sines, split(v))
     v = dot3(split(v), waves)
@@ -254,7 +254,7 @@
 
 def halves(table):
     hi = table.astype(jnp.bfloat16)
-    return hi, (table - hi.astype(np.float32)).astype(jnp.bfloat16)
+    return np.stack([hi, (table - hi.astype(np.float32)).astype(jnp.bfloat16)])
 
 
 def wall(first, number, total):
@@ -273,7 +273,7 @@
     params = pltpu.CompilerParams(vmem_limit_bytes=48 << 20)
     chunk = jax.ShapeDtypeStruct((parts, wid, 128), jnp.float32)
     t = pl.pallas_call(depth_forward_kernel, out_shape=chunk, compiler_params=params)(
-        ions, mask, *halves(sz)
+        ions, mask, halves(sz)
     )
     t = lax.all_to_all(t, ("gx", "gy"), split_axis=0, concat_axis=0, tiled=True)
     me = lax.axis_index("gx") * gy + lax.axis_index("gy")
@@ -286,7 +286,7 @@
         plane_kernel,
         out_shape=jax.ShapeDtypeStruct((gx, full_wid, 128), jnp.float32),
         compiler_params=params,
-    )(t.reshape(gx, full_wid, 128), *halves(sy), *halves(waves), scale)
+    )(t.reshape(gx, full_wid, 128), halves(sy), halves(waves), scale)
     t = lax.all_to_all(
         t.reshape(parts, wid, 128), ("gx", "gy"), split_axis=0, concat_axis=0, tiled=True
     )
@@ -294,7 +294,7 @@
         depth_back_kernel,
         out_shape=jax.ShapeDtypeStruct((length, wid, depth), jnp.float32),
         compiler_params=params,
-    )(t, *halves(sz))
+    )(t, halves(sz))
 
 
 def solve(charge):
@@ -383,7 +383,7 @@
         out_shape=[shape(9), shape(5), shape(5), shape(2), edge, edge],
         compiler_params=pltpu.CompilerParams(vmem_limit_bytes=32 << 20),
         cost_estimate=pl.CostEstimate(
-            flops=500 * cells, bytes_accessed=4 * 44 * cells, transcendentals=0
+            flops=160000 * cells, bytes_accessed=4 * 44 * cells, transcendentals=0
         ),
     )(populations, ionic[:2], ionic[2], pot)
 

time: 113 us -> 113 us (level)
    unnamed x24 -> x18, local copies, waits for them, and re-layouts: 8.96 us -> 8.28 us
where the time goes in v2:
time: 113 us; the launch traced here: 112 us
  waiting for transfers between devices  39.2 us (35%)
  Pallas kernels  32.9 us (29%)
  starting transfers between devices  26.6 us (24%)
  local copies, waits for them, and re-layouts  10.3 us (9%)
  other arithmetic  1.87 us (2%)
    pallas_call x1, Pallas kernels, body(): pl.pallas_call(collide_kernel, grid=(length,), in_specs=[block(19, same),...  17.8 us
    all_to_all x1, waiting for transfers between devices, solve_packed(): t = lax.all_to_all(t, ('gx', 'gy'), split_axis=0, concat_axis=0, tiled=True)  15.9 us
    ppermute x6, waiting for transfers between devices, up(): return lax.ppermute(x, axis, [(i, (i + 1) % n) for i in range(n)])  15.6 us
    ppermute x6, starting transfers between devices, down(): return lax.ppermute(x, axis, [((i + 1) % n, i) for i in range(n)])  14.7 us
    pallas_call x1, Pallas kernels, body(): pl.pallas_call(stream_kernel, grid=(length,), in_specs=[block(9, same), b...  8.51 us
    unnamed x18, local copies, waits for them, and re-layouts  8.28 us
    all_to_all x1, starting transfers between devices, solve_packed(): t = lax.all_to_all(t, ('gx', 'gy'), split_axis=0, concat_axis=0, tiled=True)  7.3 us
    ppermute x6, waiting for transfers between devices, down(): return lax.ppermute(x, axis, [((i + 1) % n, i) for i in range(n)])  4.99 us
  transfers between devices with their start and end apart: 14, of which 8 were waited for; matrix products, arithmetic and copies ran while one was open for 2% of the time, Pallas kernels for 0%

profile of v2, /device:TPU:0, one launch (start us, length us, event | category | flops | bytes accessed | tf_op | source)
XLA Modules:
  0.0 111.8 jit_solution(13572532207373455687)
XLA Ops:
  0.7 1.2 %copy-done = f32[2,16,32,256]{3,2,1,0:T(8,128)S(1)} copy-done((f32[2,16,32,256]{3,2,1,0:T(8,128)S(1)}, f32[2,16,32,256]{3,2,1,0:T(8,128)}, u32[]{:S(2)}) %copy-start) | copy-done | bytes 1048600
  3.9 1.6 %shard_map.103 = f32[32,32,128]{2,1,0:T(8,128)} custom-call(f32[2,16,32,256]{3,2,1,0:T(8,128)S(1)} %copy-done, s32[16,32,256]{2,1,0:T(8,128)S(1)} %copy-done.5, bf16[2,256,256]{2,1,0:T(8,128)(2,1)S(1)} %copy-done.3), custom_call_target="tpu_custom_call" | custom-call | tf_op jit(solution)/shard_map/pallas_call | solution.py:275
  5.5 7.3 %all-to-all-start = ((f32[32,32,128]{2,1,0:T(8,128)}), f32[32,32,128]{2,1,0:T(8,128)S(1)}, u32[]{:S(2)}, u32[]{:S(2)}) async-start(f32[32,32,128]{2,1,0:T(8,128)} %shard_map.103), calls=%async_computation | async-start | bytes 1048576 | tf_op jit(solution)/shard_map/all_to_all | solution.py:278
  13.2 15.9 %all-to-all-done = f32[32,32,128]{2,1,0:T(8,128)S(1)} async-done(((f32[32,32,128]{2,1,0:T(8,128)}), f32[32,32,128]{2,1,0:T(8,128)S(1)}, u32[]{:S(2)}, u32[]{:S(2)}) %all-to-all-start) | async-done | bytes 524320 | tf_op jit(solution)/shard_map/all_to_all | solution.py:278
  29.2 1.2 %copy-done.7 = bf16[2,512,512]{2,1,0:T(8,128)(2,1)S(1)} copy-done((bf16[2,512,512]{2,1,0:T(8,128)(2,1)S(1)}, bf16[2,512,512]{2,1,0:T(8,128)(2,1)}, u32[]{:S(2)}) %copy-start.7) | copy-done | bytes 1048600
  30.4 2.5 %shard_map.104 = f32[4,256,128]{2,1,0:T(8,128)} custom-call(f32[4,256,128]{2,1,0:T(8,128)S(1)} %bitcast.36, bf16[2,256,256]{2,1,0:T(8,128)(2,1)S(1)} %copy-done.4, bf16[2,512,512]{2,1,0:T(8,128)(2,1)S(1)} %copy-done.7, f32[256,512]{1,0:T(8,128)S(1)} %add_multiply_fusion.scale), custom_call_target="tpu_custom_call" | custom-call | tf_op jit(solution)/shard_map/pallas_call | solution.py:285
  32.9 2.6 %all-to-all-start.1 = ((f32[32,32,128]{2,1,0:T(8,128)}), f32[32,32,128]{2,1,0:T(8,128)S(1)}, u32[]{:S(2)}, u32[]{:S(2)}) async-start(f32[32,32,128]{2,1,0:T(8,128)} %bitcast.3), calls=%async_computation.1 | async-start | bytes 1048576 | tf_op jit(solution)/shard_map/all_to_all | solution.py:290
  35.6 1.7 %collective-permute-start = (f32[3,1,32,256]{3,2,1,0:T(8,128)S(1)}, f32[3,1,32,256]{3,2,1,0:T(8,128)S(1)}, u32[]{:S(2)}, u32[]{:S(2)}) collective-permute-start(f32[3,1,32,256]{3,2,1,0:T(8,128)S(1)} %get-tuple-element.21), channel_id=1, source_target_pairs={{0,8},{8,16},{16,24},{24,0},{1,9},{9,17},{17,25},{25,1},{2,10},{10... | collective-permute-start | bytes 294920 | tf_op jit(solution)/shard_map/ppermute | solution.py:44
  37.3 1.3 %collective-permute-start.3 = (f32[3,1,32,256]{3,2,1,0:T(8,128)S(1)}, f32[3,1,32,256]{3,2,1,0:T(8,128)S(1)}, u32[]{:S(2)}, u32[]{:S(2)}) collective-permute-start(f32[3,1,32,256]{3,2,1,0:T(8,128)S(1)} %get-tuple-element.22), channel_id=1, source_target_pairs={{8,0},{16,8},{24,16},{0,24},{9,1},{17,9},{25,17},{1,25},{10,2},{18... | collective-permute-start | bytes 294920 | tf_op jit(solution)/shard_map/ppermute | solution.py:49
  38.7 3.5 %collective-permute-start.2 = (f32[3,16,1,256]{3,2,1,0:T(1,128)S(1)}, f32[3,16,1,256]{3,2,1,0:T(1,128)S(1)}, u32[]{:S(2)}, u32[]{:S(2)}) collective-permute-start(f32[3,16,1,256]{3,2,1,0:T(1,128)S(1)} %get-tuple-element.20), channel_id=1, source_target_pairs={{1,0},{2,1},{3,2},{4,3},{5,4},{6,5},{7,6},{0,7},{9,8},{10,9},{11,1... | collective-permute-start | bytes 147464 | tf_op jit(solution)/shard_map/ppermute | solution.py:49
  42.3 7.0 %collective-permute-done.1 = f32[3,16,1,256]{3,2,1,0:T(1,128)S(1)} collective-permute-done((f32[3,16,1,256]{3,2,1,0:T(1,128)S(1)}, f32[3,16,1,256]{3,2,1,0:T(1,128)S(1)}, u32[]{:S(2)}, u32[]{:S(2)}) %collective-permute-start.1) | collective-permute-done | bytes 49184 | tf_op jit(solution)/shard_map/ppermute | solution.py:44
  49.7 2.7 %all-to-all-done.1.t = f32[32,32,128]{2,1,0:T(8,128)S(1)} async-done(((f32[32,32,128]{2,1,0:T(8,128)}), f32[32,32,128]{2,1,0:T(8,128)S(1)}, u32[]{:S(2)}, u32[]{:S(2)}) %all-to-all-start.1) | async-done | bytes 524320 | tf_op jit(solution)/shard_map/all_to_all | solution.py:290
  52.4 1.6 %shard_map.105 = f32[16,32,256]{2,1,0:T(8,128)} custom-call(f32[32,32,128]{2,1,0:T(8,128)S(1)} %all-to-all-done.1.t, bf16[2,256,256]{2,1,0:T(8,128)(2,1)S(1)} %copy-done.4), custom_call_target="tpu_custom_call" | custom-call | tf_op jit(solution)/shard_map/pallas_call | solution.py:293
  55.9 3.5 %collective-permute-start.6 = (f32[16,1,256]{2,1,0:T(1,128)S(1)}, f32[16,1,256]{2,1,0:T(1,128)S(1)}, u32[]{:S(2)}, u32[]{:S(2)}) collective-permute-start(f32[16,1,256]{2,1,0:T(1,128)S(1)} %get-tuple-element.24), channel_id=1, source_target_pairs={{1,0},{2,1},{3,2},{4,3},{5,4},{6,5},{7,6},{0,7},{9,8},{10,9},{11,1... | collective-permute-start | bytes 49160 | tf_op jit(solution)/shard_map/ppermute | solution.py:49
  59.4 2.9 %collective-permute-start.7 = (f32[1,32,256]{2,1,0:T(8,128)S(1)}, f32[1,32,256]{2,1,0:T(8,128)S(1)}, u32[]{:S(2)}, u32[]{:S(2)}) collective-permute-start(f32[1,32,256]{2,1,0:T(8,128)S(1)} %get-tuple-element.26), channel_id=1, source_target_pairs={{8,0},{16,8},{24,16},{0,24},{9,1},{17,9},{25,17},{1,25},{10,2},{18... | collective-permute-start | bytes 98312 | tf_op jit(solution)/shard_map/ppermute | solution.py:49
  62.3 1.9 %collective-permute-done.4 = f32[1,32,256]{2,1,0:T(8,128)S(1)} collective-permute-done((f32[1,32,256]{2,1,0:T(8,128)S(1)}, f32[1,32,256]{2,1,0:T(8,128)S(1)}, u32[]{:S(2)}, u32[]{:S(2)}) %collective-permute-start.4) | collective-permute-done | bytes 32800 | tf_op jit(solution)/shard_map/ppermute | solution.py:44
  65.3 3.8 %copy-done.2 = f32[19,16,32,256]{3,2,1,0:T(8,128)S(1)} copy-done((f32[19,16,32,256]{3,2,1,0:T(8,128)S(1)}, f32[19,16,32,256]{3,2,1,0:T(8,128)}, u32[]{:S(2)}) %copy-start.2) | copy-done | bytes 9961496
  70.0 17.8 %shard_map.106 = (f32[9,16,32,256]{3,2,1,0:T(8,128)S(1)}, f32[5,16,32,256]{3,2,1,0:T(8,128)S(1)}, f32[5,16,32,256]{3,2,1,0:T(8,128)S(1)}, f32[2,16,32,256]{3,2,1...) custom-call(f32[19,16,32,256]{3,2,1,0:T(8,128)} %pop.3, f32[2,18,34,256]{3,2,1,0:T(8,128)S(1)} %slice.118.ion, ...), custom_call_target="tpu_custom_call" | custom-call | flops 20971520000 | bytes 23068672 | tf_op jit(solution)/shard_map/pallas_call | solution.py:378
  87.8 3.0 %collective-permute-start.9 = (f32[5,32,256]{2,1,0:T(8,128)S(1)}, f32[5,32,256]{2,1,0:T(8,128)S(1)}, u32[]{:S(2)}, u32[]{:S(2)}) collective-permute-start(f32[5,32,256]{2,1,0:T(8,128)S(1)} %bitcast.38), channel_id=1, source_target_pairs={{8,0},{16,8},{24,16},{0,24},{9,1},{17,9},{25,17},{1,25},{10,2},{18... | collective-permute-start | bytes 491528 | tf_op jit(solution)/shard_map/ppermute | solution.py:49
  90.8 2.8 %collective-permute-done.9.hr = f32[5,32,256]{2,1,0:T(8,128)S(1)} collective-permute-done((f32[5,32,256]{2,1,0:T(8,128)S(1)}, f32[5,32,256]{2,1,0:T(8,128)S(1)}, u32[]{:S(2)}, u32[]{:S(2)}) %collective-permute-start.9) | collective-permute-done | bytes 163872 | tf_op jit(solution)/shard_map/ppermute | solution.py:49
  93.7 3.4 %collective-permute-done.8.hl = f32[5,32,256]{2,1,0:T(8,128)S(1)} collective-permute-done((f32[5,32,256]{2,1,0:T(8,128)S(1)}, f32[5,32,256]{2,1,0:T(8,128)S(1)}, u32[]{:S(2)}, u32[]{:S(2)}) %collective-permute-start.8) | collective-permute-done | bytes 163872 | tf_op jit(solution)/shard_map/ppermute | solution.py:44
  97.7 2.2 %collective-permute-done.11.ht = f32[5,16,256]{2,1,0:T(8,128)S(1)} collective-permute-done((f32[5,16,256]{2,1,0:T(8,128)S(1)}, f32[5,16,256]{2,1,0:T(8,128)S(1)}, u32[]{:S(2)}, u32[]{:S(2)}) %collective-permute-start.11) | collective-permute-done | bytes 81952 | tf_op jit(solution)/shard_map/ppermute | solution.py:49
  99.9 3.4 %collective-permute-done.10.hb = f32[5,16,256]{2,1,0:T(8,128)S(1)} collective-permute-done((f32[5,16,256]{2,1,0:T(8,128)S(1)}, f32[5,16,256]{2,1,0:T(8,128)S(1)}, u32[]{:S(2)}, u32[]{:S(2)}) %collective-permute-start.10) | collective-permute-done | bytes 81952 | tf_op jit(solution)/shard_map/ppermute | solution.py:44
  103.3 8.5 %shard_map.108 = f32[19,16,32,256]{3,2,1,0:T(8,128)} custom-call(f32[9,16,32,256]{3,2,1,0:T(8,128)S(1)} %get-tuple-element.11.p0, f32[5,16,32,256]{3,2,1,0:T(8,128)S(1)} %get-tuple-element.12.pp, f32[5,16,32,256]{3,2,1,0:T(8,128)S(1)} %get-tuple-element.13.pm, f32[5,32,256]{2,1,0:T(8,128)S(1)} %collective-permute-done.8.hl, ...), custom_call_target="tpu_custom_call" | custom-call | flops 2621440 | bytes 19922944 | tf_op jit(solution)/shard_map/pallas_call | solution.py:403
  (56 shorter events, 7.5 us)
Async XLA Ops:
  0.6 12.3 %copy-start.8 = (f32[64]{0:T(128)S(1)}, f32[64]{0:T(128)}, u32[]{:S(2)}) copy-start(f32[64]{0:T(128)} %constant.47) | copy-start | bytes 772
  0.6 1.2 %copy-start = (f32[2,16,32,256]{3,2,1,0:T(8,128)S(1)}, f32[2,16,32,256]{3,2,1,0:T(8,128)}, u32[]{:S(2)}) copy-start(f32[2,16,32,256]{3,2,1,0:T(8,128)} %ion.1) | copy-start | bytes 3145732
  1.9 0.9 copy-start.3
  2.8 1.0 copy-start.5
  3.9 25.3 %copy-start.4 = (bf16[2,256,256]{2,1,0:T(8,128)(2,1)S(1)}, bf16[2,256,256]{2,1,0:T(8,128)(2,1)}, u32[]{:S(2)}) copy-start(bf16[2,256,256]{2,1,0:T(8,128)(2,1)} %constant.36.clone.s) | copy-start | bytes 786436
  5.5 23.7 %all-to-all-start = ((f32[32,32,128]{2,1,0:T(8,128)}), f32[32,32,128]{2,1,0:T(8,128)S(1)}, u32[]{:S(2)}, u32[]{:S(2)}) async-start(f32[32,32,128]{2,1,0:T(8,128)} %shard_map.103), calls=%async_computation | async-start | bytes 1048576 | tf_op jit(solution)/shard_map/all_to_all | solution.py:278
  13.1 22.4 %copy-start.6 = (s32[16,32,256]{2,1,0:T(8,128)S(1)}, s32[16,32,256]{2,1,0:T(8,128)}, u32[]{:S(2)}) copy-start(s32[16,32,256]{2,1,0:T(8,128)} %mask.1) | copy-start | bytes 1572868
  29.2 1.2 %copy-start.7 = (bf16[2,512,512]{2,1,0:T(8,128)(2,1)S(1)}, bf16[2,512,512]{2,1,0:T(8,128)(2,1)}, u32[]{:S(2)}) copy-start(bf16[2,512,512]{2,1,0:T(8,128)(2,1)} %constant.38.clone.h) | copy-start | bytes 3145732
  30.4 5.2 %copy-start.1 = (f32[2,16,32,256]{3,2,1,0:T(8,128)S(1)}, f32[2,16,32,256]{3,2,1,0:T(8,128)}, u32[]{:S(2)}) copy-start(f32[2,16,32,256]{3,2,1,0:T(8,128)} %ion.1) | copy-start | bytes 3145732
  32.9 19.5 %all-to-all-start.1 = ((f32[32,32,128]{2,1,0:T(8,128)}), f32[32,32,128]{2,1,0:T(8,128)S(1)}, u32[]{:S(2)}, u32[]{:S(2)}) async-start(f32[32,32,128]{2,1,0:T(8,128)} %bitcast.3), calls=%async_computation.1 | async-start | bytes 1048576 | tf_op jit(solution)/shard_map/all_to_all | solution.py:290
  35.6 13.6 %collective-permute-start = (f32[3,1,32,256]{3,2,1,0:T(8,128)S(1)}, f32[3,1,32,256]{3,2,1,0:T(8,128)S(1)}, u32[]{:S(2)}, u32[]{:S(2)}) collective-permute-start(f32[3,1,32,256]{3,2,1,0:T(8,128)S(1)} %get-tuple-element.21), channel_id=1, source_target_pairs={{0,8},{8,16},{16,24},{24,0},{1,9},{9,17},{17,25},{25,1},{2,10},{10... | collective-permute-start | bytes 294920 | tf_op jit(solution)/shard_map/ppermute | solution.py:44
  37.3 11.9 %collective-permute-start.3 = (f32[3,1,32,256]{3,2,1,0:T(8,128)S(1)}, f32[3,1,32,256]{3,2,1,0:T(8,128)S(1)}, u32[]{:S(2)}, u32[]{:S(2)}) collective-permute-start(f32[3,1,32,256]{3,2,1,0:T(8,128)S(1)} %get-tuple-element.22), channel_id=1, source_target_pairs={{8,0},{16,8},{24,16},{0,24},{9,1},{17,9},{25,17},{1,25},{10,2},{18... | collective-permute-start | bytes 294920 | tf_op jit(solution)/shard_map/ppermute | solution.py:49
  38.7 10.6 %collective-permute-start.1 = (f32[3,16,1,256]{3,2,1,0:T(1,128)S(1)}, f32[3,16,1,256]{3,2,1,0:T(1,128)S(1)}, u32[]{:S(2)}, u32[]{:S(2)}) collective-permute-start(f32[3,16,1,256]{3,2,1,0:T(1,128)S(1)} %get-tuple-element.19), channel_id=1, source_target_pairs={{0,1},{1,2},{2,3},{3,4},{4,5},{5,6},{6,7},{7,0},{8,9},{9,10},{10,1... | collective-permute-start | bytes 147464 | tf_op jit(solution)/shard_map/ppermute | solution.py:44
  38.7 10.5 %collective-permute-start.2 = (f32[3,16,1,256]{3,2,1,0:T(1,128)S(1)}, f32[3,16,1,256]{3,2,1,0:T(1,128)S(1)}, u32[]{:S(2)}, u32[]{:S(2)}) collective-permute-start(f32[3,16,1,256]{3,2,1,0:T(1,128)S(1)} %get-tuple-element.20), channel_id=1, source_target_pairs={{1,0},{2,1},{3,2},{4,3},{5,4},{6,5},{7,6},{0,7},{9,8},{10,9},{11,1... | collective-permute-start | bytes 147464 | tf_op jit(solution)/shard_map/ppermute | solution.py:49
  55.0 7.3 %collective-permute-start.5 = (f32[16,1,256]{2,1,0:T(1,128)S(1)}, f32[16,1,256]{2,1,0:T(1,128)S(1)}, u32[]{:S(2)}, u32[]{:S(2)}) collective-permute-start(f32[16,1,256]{2,1,0:T(1,128)S(1)} %get-tuple-element.23), channel_id=1, source_target_pairs={{0,1},{1,2},{2,3},{3,4},{4,5},{5,6},{6,7},{7,0},{8,9},{9,10},{10,1... | collective-permute-start | bytes 49160 | tf_op jit(solution)/shard_map/ppermute | solution.py:44
  55.9 6.5 %collective-permute-start.6 = (f32[16,1,256]{2,1,0:T(1,128)S(1)}, f32[16,1,256]{2,1,0:T(1,128)S(1)}, u32[]{:S(2)}, u32[]{:S(2)}) collective-permute-start(f32[16,1,256]{2,1,0:T(1,128)S(1)} %get-tuple-element.24), channel_id=1, source_target_pairs={{1,0},{2,1},{3,2},{4,3},{5,4},{6,5},{7,6},{0,7},{9,8},{10,9},{11,1... | collective-permute-start | bytes 49160 | tf_op jit(solution)/shard_map/ppermute | solution.py:49
  59.4 4.8 %collective-permute-start.4 = (f32[1,32,256]{2,1,0:T(8,128)S(1)}, f32[1,32,256]{2,1,0:T(8,128)S(1)}, u32[]{:S(2)}, u32[]{:S(2)}) collective-permute-start(f32[1,32,256]{2,1,0:T(8,128)S(1)} %get-tuple-element.25), channel_id=1, source_target_pairs={{0,8},{8,16},{16,24},{24,0},{1,9},{9,17},{17,25},{25,1},{2,10},{10... | collective-permute-start | bytes 98312 | tf_op jit(solution)/shard_map/ppermute | solution.py:44
  59.4 4.8 %collective-permute-start.7 = (f32[1,32,256]{2,1,0:T(8,128)S(1)}, f32[1,32,256]{2,1,0:T(8,128)S(1)}, u32[]{:S(2)}, u32[]{:S(2)}) collective-permute-start(f32[1,32,256]{2,1,0:T(8,128)S(1)} %get-tuple-element.26), channel_id=1, source_target_pairs={{8,0},{16,8},{24,16},{0,24},{9,1},{17,9},{25,17},{1,25},{10,2},{18... | collective-permute-start | bytes 98312 | tf_op jit(solution)/shard_map/ppermute | solution.py:49
  65.3 3.8 %copy-start.2 = (f32[19,16,32,256]{3,2,1,0:T(8,128)S(1)}, f32[19,16,32,256]{3,2,1,0:T(8,128)}, u32[]{:S(2)}) copy-start(f32[19,16,32,256]{3,2,1,0:T(8,128)} %pop.3) | copy-start | bytes 29884420
  87.8 5.8 %collective-permute-start.9 = (f32[5,32,256]{2,1,0:T(8,128)S(1)}, f32[5,32,256]{2,1,0:T(8,128)S(1)}, u32[]{:S(2)}, u32[]{:S(2)}) collective-permute-start(f32[5,32,256]{2,1,0:T(8,128)S(1)} %bitcast.38), channel_id=1, source_target_pairs={{8,0},{16,8},{24,16},{0,24},{9,1},{17,9},{25,17},{1,25},{10,2},{18... | collective-permute-start | bytes 491528 | tf_op jit(solution)/shard_map/ppermute | solution.py:49
  90.8 6.2 %collective-permute-start.8 = (f32[5,32,256]{2,1,0:T(8,128)S(1)}, f32[5,32,256]{2,1,0:T(8,128)S(1)}, u32[]{:S(2)}, u32[]{:S(2)}) collective-permute-start(f32[5,32,256]{2,1,0:T(8,128)S(1)} %bitcast.37), channel_id=1, source_target_pairs={{0,8},{8,16},{16,24},{24,0},{1,9},{9,17},{17,25},{25,1},{2,10},{10... | collective-permute-start | bytes 491528 | tf_op jit(solution)/shard_map/ppermute | solution.py:44
  97.1 2.8 %collective-permute-start.11 = (f32[5,16,256]{2,1,0:T(8,128)S(1)}, f32[5,16,256]{2,1,0:T(8,128)S(1)}, u32[]{:S(2)}, u32[]{:S(2)}) collective-permute-start(f32[5,16,256]{2,1,0:T(8,128)S(1)} %pad_maximum_fusion.3), channel_id=1, source_target_pairs={{1,0},{2,1},{3,2},{4,3},{5,4},{6,5},{7,6},{0,7},{9,8},{10,9},{11,1... | collective-permute-start | bytes 245768 | tf_op jit(solution)/shard_map/ppermute | solution.py:49
  97.5 5.7 %collective-permute-start.10 = (f32[5,16,256]{2,1,0:T(8,128)S(1)}, f32[5,16,256]{2,1,0:T(8,128)S(1)}, u32[]{:S(2)}, u32[]{:S(2)}) collective-permute-start(f32[5,16,256]{2,1,0:T(8,128)S(1)} %pad_maximum_fusion.2), channel_id=1, source_target_pairs={{0,1},{1,2},{2,3},{3,4},{4,5},{5,6},{6,7},{7,0},{8,9},{9,10},{10,1... | collective-permute-start | bytes 245768 | tf_op jit(solution)/shard_map/ppermute | solution.py:44
